TPU v7x, 32 devices: a whole 2x2x4 slice. The times are simulated.
32 devices in a mesh: dp: 4 (over y, x), ctx: 4 (over z), mp: 2 (over core).
Axes of the slice: x: 2, y: 2, z: 4, core: 2. Of those that a mesh axis runs over, the one named last changes fastest.
Arguments:
- streams: bfloat16 [2048, 3, 1536], P(('dp', 'ctx'), None, 'mp'), parts along dimension 0, may hold values from -6 to 6
- short_taps: float32 [7, 3, 96], P(None, None, 'mp'), may hold values from -2.5 to 2.5
- modal_residue: float32 [16, 96], P(None, 'mp'), may hold values from -0.09 to 0.09
- modal_rate: float32 [16, 96], P(None, 'mp'), may hold values from 9.765625e-05 to 0.03
- skip_gain: float32 [1536], P('mp'), may hold values from -4 to 4
- queries: bfloat16 [2048, 16, 128], P(('dp', 'ctx'), 'mp'), parts along dimension 0, may hold values from -9 to 9
- keys: bfloat16 [2048, 2, 128], P(('dp', 'ctx'), 'mp'), parts along dimension 0, may hold values from -9 to 9
- values: bfloat16 [2048, 2, 128], P(('dp', 'ctx'), 'mp'), parts along dimension 0, may hold values from -6 to 6
Outputs:
- hyena_out: bfloat16 [2048, 1536], P(('dp', 'ctx'), 'mp'), parts along dimension 0
- attn_out: bfloat16 [2048, 16, 128], P(('dp', 'ctx'), 'mp'), parts along dimension 0
There are 4 independent parts, one for each index of `dp`. A program takes and returns all parts, laid end to end along the dimension named above; an argument that names none is the same for every part. Nothing has to cross between parts.
All inputs are finite; a program needn't handle non-finite values.
Results may differ from a plain program's by a relative error of at most 0.01.
Values may be sent and summed in bfloat16 or wider, within the bound.
A program may use at most 64 MiB of HBM per device.

v0:
```python
import math

import jax
import jax.numpy as jnp
from jax import lax
from jax.sharding import PartitionSpec as P

GSIZE = 16


def shifted(value, axis, steps):
    count = lax.axis_size(axis)
    initial, last = (max(0, -steps), min(count, count - steps))
    return lax.ppermute(value, axis, [(source, source + steps) for source in range(initial, last)])


def body(streams, short_taps, modal_residue, modal_rate, skip_gain, queries, keys, values):
    tok_rows = streams.shape[0]
    reach = short_taps.shape[0] - 1
    groups_dev = modal_rate.shape[1]
    rim = shifted(streams[tok_rows - reach :], "ctx", 1)
    extended = jnp.concatenate([rim, streams], axis=0).astype(jnp.float32)
    taps_full = jnp.repeat(short_taps, GSIZE, axis=2)
    filtered = jnp.zeros(streams.shape, jnp.float32)
    for offset in range(reach + 1):
        filtered = (
            filtered + taps_full[offset] * extended[reach - offset : reach - offset + tok_rows]
        )
    gated = (filtered[:, 1] * filtered[:, 2]).astype(jnp.bfloat16)
    gated_float = gated.astype(jnp.float32).reshape(tok_rows, groups_dev, GSIZE)
    anchor = lax.axis_index("ctx") * tok_rows
    anchor_float = anchor.astype(jnp.float32)
    highest = lax.Precision.HIGHEST
    piece = lax.all_gather(gated, "ctx", axis=0, tiled=True)
    count = piece.shape[0]
    lag = anchor_float - jnp.arange(count, dtype=jnp.int32).astype(jnp.float32)
    decay = jnp.exp(-modal_rate[:, :, None] * jnp.maximum(lag, 0.0)[None, None, :])
    decay = jnp.where(lag[None, None, :] > 0.0, decay, 0.0)
    source = piece.astype(jnp.float32).reshape(count, groups_dev, GSIZE)
    state = jnp.einsum("ngs,sgc->ngc", decay, source, precision=highest)
    positions = jnp.arange(tok_rows, dtype=jnp.int32)
    coeff = modal_residue[:, :, None] * jnp.exp(
        -modal_rate[:, :, None] * positions.astype(jnp.float32)[None, None, :]
    )
    far_term = jnp.einsum("ngt,ngc->tgc", coeff, state, precision=highest)
    table = jnp.sum(coeff, axis=0)
    offsets = positions[:, None] - positions[None, :]
    toeplitz = jnp.where(offsets[None] >= 0, jnp.take(table, jnp.maximum(offsets, 0), axis=1), 0.0)
    near_term = jnp.einsum("gts,sgc->tgc", toeplitz, gated_float, precision=highest)
    long_term = (far_term + near_term).reshape(tok_rows, -1)
    hyena_out = (filtered[:, 0] * (long_term + skip_gain * gated.astype(jnp.float32))).astype(
        jnp.bfloat16
    )
    heads_dev = queries.shape[1]
    head_size = queries.shape[2]
    scale = 1.0 / math.sqrt(head_size)
    target = anchor + positions
    last_target = anchor + tok_rows - 1
    start_state = (
        jnp.full((heads_dev, tok_rows), -1e30, jnp.float32),
        jnp.zeros((heads_dev, tok_rows), jnp.float32),
        jnp.zeros((heads_dev, tok_rows, head_size), jnp.float32),
    )
    piece = (
        lax.all_gather(keys, "ctx", axis=0, tiled=True),
        lax.all_gather(values, "ctx", axis=0, tiled=True),
    )
    key_rows = piece[0][:, 0]
    value_rows = piece[1][:, 0]
    count = key_rows.shape[0]
    if count <= 512:
        span = count
    elif count % 512 == 0:
        span = 512
    else:
        span = tok_rows

    def visit(number, inner):
        begin = number * span

        def update(state_in):
            largest, total, accum = state_in
            key_block = lax.dynamic_slice_in_dim(key_rows, begin, span, 0)
            value_block = lax.dynamic_slice_in_dim(value_rows, begin, span, 0)
            source = begin + jnp.arange(span, dtype=jnp.int32)
            scores = (
                jnp.einsum("thd,sd->hts", queries, key_block, preferred_element_type=jnp.float32)
                * scale
            )
            visible = source[None, None, :] <= target[None, :, None]
            masked = jnp.where(visible, scores, -1e30)
            renewed = jnp.maximum(largest, jnp.max(masked, axis=-1))
            correction = jnp.exp(largest - renewed)
            weights = jnp.where(visible, jnp.exp(scores - renewed[..., None]), 0.0)
            total = total * correction + jnp.sum(weights, axis=-1)
            mixed = jnp.einsum(
                "hts,sd->htd",
                weights.astype(jnp.bfloat16),
                value_block,
                preferred_element_type=jnp.float32,
            )
            accum = accum * correction[..., None] + mixed
            return (renewed, total, accum)

        def unchanged(state_in):
            return state_in

        return lax.cond(begin <= last_target, update, unchanged, inner)

    largest, total, accum = lax.fori_loop(0, count // span, visit, start_state)
    attn_out = jnp.transpose(accum / total[..., None], (1, 0, 2)).astype(jnp.bfloat16)
    return (hyena_out, attn_out)


def solution(mesh):
    in_specs = (
        P(("dp", "ctx"), None, "mp"),
        P(None, None, "mp"),
        P(None, "mp"),
        P(None, "mp"),
        P("mp"),
        P(("dp", "ctx"), "mp", None),
        P(("dp", "ctx"), "mp", None),
        P(("dp", "ctx"), "mp", None),
    )
    out_specs = (P(("dp", "ctx"), "mp"), P(("dp", "ctx"), "mp", None))
    return jax.shard_map(body, mesh=mesh, in_specs=in_specs, out_specs=out_specs, check_vma=False)
```

profile of v0, /device:TPU:0, one launch (start us, length us, event | category | flops | bytes accessed | tf_op | source)
XLA Modules:
  0.0 132.1 jit_solution(5208962936751774175)
XLA Ops:
  0.6 0.8 slice.84
  1.4 4.9 %collective-permute-start = (bf16[6,3,768]{2,0,1:T(8,128)(2,1)S(1)}, bf16[6,3,768]{2,0,1:T(8,128)(2,1)S(1)}, u32[]{:S(2)}, u32[]{:S(2)}) collective-permute-start(bf16[6,3,768]{2,0,1:T(8,128)(2,1)S(1)} %slice.84), channel_id=1, source_target_pairs={{0,2},{2,4},{4,6},{1,3},{3,5},{5,7},{8,10},{10,12},{12,14},{9,11},... | collective-permute-start | bytes 82952 | tf_op jit(solution)/shard_map/ppermute | solution.py:14
  6.4 1.0 fusion.60
  7.4 0.7 neg.5
  8.2 0.8 copy.34
  9.0 14.2 %all_gather.10 = bf16[512,1,128]{2,0,1:T(8,128)(2,1)S(1)} all-gather(bf16[128,1,128]{2,0,1:T(8,128)(2,1)} %param.16), channel_id=1, replica_groups=mesh['dp'=4,'ctx'=4,'mp'=2] {'ctx'}, dimensions={0}, use_global_device_ids=true | all-gather | bytes 163840 | tf_op jit(solution)/shard_map/all_gather | solution.py:65
  23.2 13.5 %all_gather.11 = bf16[512,1,128]{2,0,1:T(8,128)(2,1)S(1)} all-gather(bf16[128,1,128]{2,0,1:T(8,128)(2,1)} %param.17), channel_id=1, replica_groups=mesh['dp'=4,'ctx'=4,'mp'=2] {'ctx'}, dimensions={0}, use_global_device_ids=true | all-gather | bytes 163840 | tf_op jit(solution)/shard_map/all_gather | solution.py:66
  36.8 3.0 %conditional.1 = (f32[8,128]{1,0:T(8,128)S(1)}, f32[8,128,128]{2,0,1:T(8,128)S(1)}) conditional(s32[]{:T(128)} %convert_element_type.65, (f32[8,128]{1,0:T(8,128)S(1)}, f32[8,128,128]{2,1,0:T(8,128)S(1)}) %tuple.25, (s32[]{:T(128)}, s32[128]{0:T(128)S(1)}, bf16[512,1,128]{2,0,1:T(8,128)(2,1)S(1)}, bf16[128,8,128]{2,1,0:T(8,128)(2,1)}, ...), branch_computations={%region_1.2_spmd, %region_2.5_spmd} | conditional | flops 274533504 | bytes 9225748 | solution.py:108
  36.8 1.5 %fusion = (f32[8,128]{1,0:T(8,128)S(1)}, f32[512,128,8]{1,0,2:T(8,128)S(1)}) fusion(pred[128,512]{0,1:T(8,128)(4,1)S(1)} %iota_compare_fusion, bf16[128,8,128]{2,1,0:T(8,128)(2,1)} %get-tuple-element.122, bf16[512,1,128]{2,0,1:T(8,128)(2,1)S(1)} %get-tuple-element.91), kind=kOutput, calls=%fused_computation.3 | convolution fusion | flops 135789568 | bytes 2560000 | tf_op jit(solution)/shard_map/while/body/eval_jaxpr/cond/branch_1_fun/thd,sd->hts/dot_general | solution.py:87
  38.3 0.4 fusion.4
  38.8 0.7 convolution_add_fusion
  39.5 0.3 copy.44
  39.9 0.9 fusion.50
  40.8 0.3 fusion.48
  41.1 1.1 copy.32
  42.5 0.1 broadcast_in_dim.120
  42.7 0.1 broadcast_in_dim.122
  42.9 0.1 broadcast_in_dim.124
  43.1 0.1 broadcast_in_dim.126
  43.3 0.1 broadcast_in_dim.128
  43.5 0.1 broadcast_in_dim.116
  43.7 54.8 %gather_fusion = f32[16384,48]{1,0:T(8,128)} fusion(f32[48,128]{0,1:T(8,128)S(1)} %copy.36, s32[16384]{0:T(1024)S(1)} %bitcast_clamp_fusion), kind=kCustom, calls=%fused_computation | custom fusion | bytes 6356992 | tf_op jit(solution)/shard_map/jit(_take)/gather | solution.py:48
  98.4 5.8 %copy.37 = f32[128,128,48]{1,0,2:T(8,128)S(1)} copy(f32[128,128,48]{2,1,0:T(8,128)} %bitcast.69) | data formatting | bytes 6291456 | tf_op jit(solution)/shard_map/jit(_take)/gather | solution.py:48
  104.2 1.1 copy.31
  105.4 1.7 %maximum_convert_fusion = f32[134,3,768]{0,2,1:T(8,128)S(1)} fusion(bf16[128,3,768]{0,2,1:T(8,128)(2,1)} %copy.32, bf16[6,3,768]{0,2,1:T(8,128)(2,1)} %copy.31), kind=kLoop, calls=%fused_computation.51 | loop fusion | flops 1234944 | bytes 1852416 | tf_op jit(solution)/shard_map/convert_element_type | solution.py:22
  107.1 4.4 %fusion.34 = f32[128,3,768]{0,2,1:T(8,128)S(1)} fusion(f32[134,3,768]{0,2,1:T(8,128)S(1)} %maximum_convert_fusion, f32[3,768]{1,0:T(4,128)S(1)} %broadcast_in_dim.128, f32[3,768]{1,0:T(4,128)S(1)} %broadcast_in_dim.126, f32[3,768]{1,0:T(4,128)S(1)} %broadcast_in_dim.124, f32[3,768]{1,0:T(4,128)S(1)} %broadcast_in_dim.122, ...), kind=kLoop, calls=%fused_computation.39 | loop fusion | flops 3833856 | bytes 9501696 | tf_op jit(solution)/shard_map/add | solution.py:27
  111.5 14.9 %all-gather = bf16[512,1,768]{0,2,1:T(8,128)(2,1)S(1)} all-gather(bf16[128,1,768]{0,2,1:T(8,128)(2,1)S(1)} %fusion.44), channel_id=2, replica_groups=mesh['dp'=4,'ctx'=4,'mp'=2] {'ctx'}, dimensions={0}, use_global_device_ids=true | all-gather | bytes 983040 | tf_op jit(solution)/shard_map/all_gather | solution.py:34
  126.4 1.4 %fusion.28 = f32[16,48,16]{0,2,1:T(8,128)S(1)} fusion(bf16[512,48,16]{0,2,1:T(8,128)(2,1)S(1)} %bitcast.71, f32[512]{0:T(512)S(1)} %fusion.55, f32[16,48]{0,1:T(8,128)S(1)} %copy.33, pred[512]{0:T(512)(128)(4,1)S(1)} %fusion.56), kind=kOutput, calls=%fused_computation.36 | convolution fusion | flops 76283904 | bytes 841216 | tf_op jit(solution)/shard_map/ngs,sgc->ngc/dot_general | solution.py:40
  127.8 0.6 fusion.49
  128.5 2.6 %fusion.31 = f32[48,16,128]{2,1,0:T(8,128)S(1)} fusion(f32[48,16,128]{2,1,0:T(8,128)S(1)} %fusion.49, bf16[128,48,16]{0,2,1:T(8,128)(2,1)S(1)} %bitcast.70, f32[128,128,48]{1,0,2:T(8,128)S(1)} %copy.37, pred[128,128]{1,0:T(8,128)(4,1)S(1)} %get-tuple-element.149, pred[128,128]{1,0:T(8,128)(4,1)S(1)} %get-tuple-element.148), kind=kOutput, calls=%fused_computation.37 | convolution fusion | flops 152666112 | bytes 4161536 | tf_op jit(solution)/shard_map/gts,sgc->tgc/dot_general | solution.py:49
  131.1 0.2 fusion.46
  131.3 0.8 copy.41
  (33 shorter events, 1.2 us)
Async XLA Ops:
  1.4 102.8 %collective-permute-start = (bf16[6,3,768]{2,0,1:T(8,128)(2,1)S(1)}, bf16[6,3,768]{2,0,1:T(8,128)(2,1)S(1)}, u32[]{:S(2)}, u32[]{:S(2)}) collective-permute-start(bf16[6,3,768]{2,0,1:T(8,128)(2,1)S(1)} %slice.84), channel_id=1, source_target_pairs={{0,2},{2,4},{4,6},{1,3},{3,5},{5,7},{8,10},{10,12},{12,14},{9,11},... | collective-permute-start | bytes 82952 | tf_op jit(solution)/shard_map/ppermute | solution.py:14
  36.8 4.4 %copy-start = (bf16[128,3,768]{2,0,1:T(8,128)(2,1)S(1)}, bf16[128,3,768]{2,0,1:T(8,128)(2,1)}, u32[]{:S(2)}) copy-start(bf16[128,3,768]{2,0,1:T(8,128)(2,1)} %param.10) | copy-start | bytes 1769476
  128.5 2.6 %copy-start.1 = (f32[768]{0:T(1024)S(1)}, f32[768]{0:T(1024)}, u32[]{:S(2)}) copy-start(f32[768]{0:T(1024)} %param.14) | copy-start | bytes 9220
where the time goes:
time: 133 us; the launch traced here: 132 us
  local copies, waits for them, and re-layouts  68.1 us (51%)
  blocking collectives  42.6 us (32%)
  other arithmetic  8.85 us (7%)
  matrix products  6.77 us (5%)
  starting transfers between devices  4.93 us (4%)
    gather x2, local copies, waits for them, and re-layouts, body(): jnp.take(table, jnp.maximum(offsets, 0), axis=1)  60.5 us
    all_gather x1, blocking collectives, body(): piece = lax.all_gather(gated, 'ctx', axis=0, tiled=True)  14.9 us
    all_gather x1, blocking collectives, body(): lax.all_gather(keys, 'ctx', axis=0, tiled=True)  14.2 us
    all_gather x1, blocking collectives, body(): lax.all_gather(values, 'ctx', axis=0, tiled=True)  13.5 us
    ppermute x1, starting transfers between devices, shifted(): lax.ppermute(value, axis, [(source, source + steps) for source in range(i...  4.93 us
    add x1, other arithmetic, body(): filtered + taps_full[offset] * extended[reach - offset:reach - offset + t...  4.42 us
    unnamed x11, local copies, waits for them, and re-layouts  2.73 us
  transfers between devices with their start and end apart: 1, of which 0 were waited for; matrix products, arithmetic and copies ran while one was open for 53% of the time, Pallas kernels for 0%

commit v1 on v0

v1 whole, which is shorter than its diff:
```python
import functools
import math

import jax
import jax.numpy as jnp
from jax import lax
from jax.experimental import pallas as pl
from jax.experimental.pallas import tpu as pltpu
from jax.sharding import PartitionSpec as P

GSIZE = 16
LANES = 128
EDGE = 8
HEAD_ROWS = 16
MESH = pl.DeviceIdType.MESH
BF16 = jnp.bfloat16
F32 = jnp.float32


def iota(shape, axis):
    return lax.broadcasted_iota(jnp.int32, shape, axis)


def dot(a, b):
    return jnp.dot(a, b, preferred_element_type=F32)


def dot_nt(a, b):
    return lax.dot_general(a, b, (((1,), (1,)), ((), ())), preferred_element_type=F32)


def split_hi_lo(value):
    high = value.astype(BF16)
    return high, (value - high.astype(F32)).astype(BF16)


def kernel(
    n, heads, chunk,
    streams, taps, residue, rate, skip, q_in, k_in, v_in,
    hy_out, at_out,
    xs, qv, kv, rim_tx, rim_rx, ext, gated, tapx, decay, coeff, toep, longt, gate,
    st_tx, st_rx, acc, big, hy_v, at_v,
    in_sem, out_sem, kv_send, kv_recv, rim_send, rim_recv, st_send, st_recv,
):
    me = lax.axis_index("ctx")
    rows, chans = xs.shape[1], xs.shape[2]
    modes, groups = rate.shape
    reach = taps.shape[1] - 1
    tiles = chans // LANES
    per = LANES // GSIZE
    half = chans // 2

    in_copies = [
        pltpu.make_async_copy(streams, xs, in_sem.at[0]),
        pltpu.make_async_copy(k_in, kv.at[me, 0], in_sem.at[1]),
        pltpu.make_async_copy(v_in, kv.at[me, 1], in_sem.at[2]),
        pltpu.make_async_copy(q_in, qv, in_sem.at[3]),
    ]
    for copy in in_copies:
        copy.start()

    barrier = pltpu.get_barrier_semaphore()
    for d in range(1, n):
        @pl.when(me >= d)
        def _():
            pl.semaphore_signal(barrier, inc=1, device_id={"ctx": me - d}, device_id_type=MESH)

    def kv_copy(part, d):
        src = k_in if part == 0 else v_in
        return pltpu.make_async_remote_copy(
            src_ref=src, dst_ref=kv.at[me, part], send_sem=kv_send.at[d, part],
            recv_sem=kv_recv.at[me, part], device_id={"ctx": me + d}, device_id_type=MESH)

    def kv_arrival(part, source):
        return pltpu.make_async_remote_copy(
            src_ref=kv.at[source, part], dst_ref=kv.at[source, part], send_sem=kv_send.at[0, part],
            recv_sem=kv_recv.at[source, part], device_id={"ctx": source}, device_id_type=MESH)

    def st_copy(d):
        return pltpu.make_async_remote_copy(
            src_ref=st_tx, dst_ref=st_rx.at[me], send_sem=st_send.at[d],
            recv_sem=st_recv.at[me], device_id={"ctx": me + d}, device_id_type=MESH)

    def st_arrival(source):
        return pltpu.make_async_remote_copy(
            src_ref=st_tx, dst_ref=st_rx.at[source], send_sem=st_send.at[0],
            recv_sem=st_recv.at[source], device_id={"ctx": source}, device_id_type=MESH)

    def rim_copy():
        return pltpu.make_async_remote_copy(
            src_ref=rim_tx, dst_ref=rim_rx, send_sem=rim_send, recv_sem=rim_recv,
            device_id={"ctx": lax.rem(me + 1, n)}, device_id_type=MESH)

    in_copies[0].wait()
    tail = xs[:, rows - HEAD_ROWS:, :].astype(F32)[:, HEAD_ROWS - EDGE:, :]
    rim_tx[:, :chans] = jnp.concatenate([tail[1], tail[2]], axis=0).astype(BF16)
    rim_tx[:, chans:] = jnp.concatenate([tail[0, :, :half], tail[0, :, half:]], axis=0).astype(BF16)

    @pl.when(me < n - 1)
    def _():
        pl.semaphore_wait(barrier, n - 1 - me)
        rim_copy().start()

    for d in range(1, n):
        @pl.when(me + d < n)
        def _():
            kv_copy(0, d).start()
            kv_copy(1, d).start()

    spread = (iota((groups, chans), 1) // GSIZE == iota((groups, chans), 0)).astype(F32)
    highest = lax.Precision.HIGHEST
    for j in range(3):
        tapx[j, : reach + 1, :] = jnp.dot(
            taps[j], spread, precision=highest, preferred_element_type=F32)
    rate_nc = jnp.dot(rate[...], spread, precision=highest, preferred_element_type=F32)
    step_decay = jnp.exp(rate_nc * (-float(rows)))

    for j in range(3):
        for q in range(tiles):
            ext[j * tiles + q, EDGE:, :] = xs[j, :, q * LANES:(q + 1) * LANES].astype(F32)

    def filtered(j, q, low, high):
        total = None
        for k in range(reach + 1):
            term = (tapx[j, k:k + 1, q * LANES:(q + 1) * LANES]
                    * ext[j * tiles + q, pl.ds(EDGE - k + low, high - low), :])
            total = term if total is None else total + term
        return total

    def fill_gated(low, high):
        for q in range(tiles):
            gated[low:high, q * LANES:(q + 1) * LANES] = (
                filtered(1, q, low, high) * filtered(2, q, low, high)).astype(BF16)

    fill_gated(HEAD_ROWS, rows)

    lane = iota((modes, LANES), 1).astype(F32)
    causal = iota((rows, LANES), 1) <= iota((rows, LANES), 0)
    rate_v = rate[...]
    residue_v = residue[...]
    for g in range(groups):
        rate_b = jnp.broadcast_to(rate_v[:, g:g + 1], (modes, LANES))
        residue_b = jnp.broadcast_to(residue_v[:, g:g + 1], (modes, LANES))
        fall = jnp.exp(rate_b * (lane - (rows - 1.0)))
        high, low = split_hi_lo(fall)
        q, gg = g // per, g % per
        decay[q, gg * modes:(gg + 1) * modes, :] = high
        decay[q, LANES + gg * modes:LANES + (gg + 1) * modes, :] = low
        coeff[q, gg * modes:(gg + 1) * modes, :] = residue_b * jnp.exp(rate_b * (-1.0 - lane))
        table = jnp.sum(residue_b * fall, axis=0, keepdims=True)
        rolled = pltpu.roll(jnp.broadcast_to(table, (rows, LANES)), 1, 1, stride=1, stride_axis=0)
        toep[q, :, gg * LANES:(gg + 1) * LANES] = jnp.where(causal, rolled, 0.0).astype(BF16)

    @pl.when(me > 0)
    def _():
        rim_copy().wait_recv()
        edge = rim_rx[...].astype(F32)
        for q in range(tiles):
            cut = slice(q * LANES, (q + 1) * LANES)
            ext[tiles + q, :EDGE, :] = edge[:EDGE, cut]
            ext[2 * tiles + q, :EDGE, :] = edge[EDGE:, cut]
            place, row = (q, 0) if q < tiles // 2 else (q - tiles // 2, EDGE)
            ext[q, :EDGE, :] = edge[row:row + EDGE, chans + place * LANES:chans + (place + 1) * LANES]

    @pl.when(me == 0)
    def _():
        ext[:, :EDGE, :] = jnp.zeros((3 * tiles, EDGE, LANES), F32)

    fill_gated(0, HEAD_ROWS)

    pick = iota((modes, LANES), 1) // GSIZE
    for q in range(tiles):
        cut = slice(q * LANES, (q + 1) * LANES)
        full = dot(decay[q], gated[:, cut])
        state = jnp.zeros((modes, LANES), F32)
        for gg in range(per):
            both = (full[gg * modes:(gg + 1) * modes]
                    + full[LANES + gg * modes:LANES + (gg + 1) * modes])
            state = jnp.where(pick == gg, both, state)
        st_tx[:, cut] = state

    for d in range(1, n):
        @pl.when(me + d < n)
        def _():
            st_copy(d).start()

    pick_rows = iota((rows, LANES), 1) // GSIZE
    for q in range(tiles):
        cut = slice(q * LANES, (q + 1) * LANES)
        own = gated[:, cut]
        parts = jnp.concatenate(
            [jnp.where(pick_rows == gg, own, jnp.zeros_like(own)) for gg in range(per)], axis=0)
        longt[:, cut] = dot(toep[q], parts) + skip[:, cut] * own.astype(F32)
        gate[:, cut] = filtered(0, q, 0, rows)

    scale = math.log2(math.e) / math.sqrt(LANES)
    for copy in in_copies[1:]:
        copy.wait()
    ones = jnp.ones((rows, LANES), BF16)
    wide = heads * rows

    own_value = jnp.concatenate([kv[me, 1], ones], axis=1)
    own_key = kv[me, 0]
    for c in range(wide // chunk):
        cut = slice(c * chunk, (c + 1) * chunk)
        scores = dot_nt(qv[cut, :], own_key) * scale
        target = (iota((chunk, LANES), 0) + c * chunk) // heads
        scores = jnp.where(iota((chunk, LANES), 1) <= target, scores, -1e30)
        largest = jnp.broadcast_to(jnp.max(scores, axis=1, keepdims=True), (chunk, LANES))
        weights = jnp.exp2(scores - largest).astype(BF16)
        big[cut, :] = largest
        acc[cut, :] = dot(weights, own_value)

    def far_block(d, carry):
        source = me - d
        kv_arrival(0, source).wait_recv()
        kv_arrival(1, source).wait_recv()
        value = jnp.concatenate([kv[source, 1], ones], axis=1)
        key = kv[source, 0]
        for c in range(wide // chunk):
            cut = slice(c * chunk, (c + 1) * chunk)
            scores = dot_nt(qv[cut, :], key) * scale
            before = big[cut, :]
            largest = jnp.maximum(before, jnp.max(scores, axis=1, keepdims=True))
            weights = jnp.exp2(scores - largest).astype(BF16)
            fix = jnp.exp2(before - largest)
            big[cut, :] = largest
            acc[cut, :] = acc[cut, :] * jnp.concatenate([fix, fix], axis=1) + dot(weights, value)
        return carry

    lax.fori_loop(1, me + 1, far_block, 0)

    for c in range(wide // chunk):
        cut = slice(c * chunk, (c + 1) * chunk)
        at_v[cut, :] = (acc[cut, :LANES] / acc[cut, LANES:]).astype(BF16)
    at_copy = pltpu.make_async_copy(at_v, at_out, out_sem.at[0])
    at_copy.start()

    def gather_state(source, state):
        st_arrival(source).wait_recv()
        return state * step_decay + st_rx[source]

    state = lax.fori_loop(0, me, gather_state, jnp.zeros((modes, chans), F32))
    for q in range(tiles):
        cut = slice(q * LANES, (q + 1) * LANES)
        block = jnp.concatenate(
            [jnp.where(pick == gg, state[:, cut], 0.0) for gg in range(per)], axis=0)
        s_high, s_low = split_hi_lo(block)
        c_high, c_low = split_hi_lo(jnp.transpose(coeff[q]))
        far = dot(jnp.concatenate([c_high, c_low, c_high], axis=1),
                  jnp.concatenate([s_high, s_high, s_low], axis=0))
        hy_v[:, cut] = (gate[:, cut] * (longt[:, cut] + far)).astype(BF16)
    hy_copy = pltpu.make_async_copy(hy_v, hy_out, out_sem.at[1])
    hy_copy.start()

    @pl.when(me < n - 1)
    def _():
        rim_copy().wait_send()

    for d in range(1, n):
        @pl.when(me + d < n)
        def _():
            kv_copy(0, d).wait_send()
            kv_copy(1, d).wait_send()
            st_copy(d).wait_send()
    at_copy.wait()
    hy_copy.wait()


def body(n, streams, short_taps, modal_residue, modal_rate, skip_gain, queries, keys, values):
    rows, _, chans = streams.shape
    heads, size = queries.shape[1], queries.shape[2]
    modes, groups = modal_rate.shape
    tiles = chans // LANES
    per = LANES // GSIZE
    wide = heads * rows
    chunk = min(256, wide)
    reach = short_taps.shape[0]
    vmem, hbm = pl.BlockSpec(memory_space=pltpu.VMEM), pl.BlockSpec(memory_space=pl.ANY)
    dma = pltpu.SemaphoreType.DMA
    hyena, attn = pl.pallas_call(
        functools.partial(kernel, n, heads, chunk),
        out_shape=(jax.ShapeDtypeStruct((rows, chans), BF16),
                   jax.ShapeDtypeStruct((wide, size), BF16)),
        in_specs=[hbm, vmem, vmem, vmem, vmem, hbm, hbm, hbm],
        out_specs=(hbm, hbm),
        scratch_shapes=[
            pltpu.VMEM((3, rows, chans), BF16),
            pltpu.VMEM((wide, size), BF16),
            pltpu.VMEM((n, 2, rows, size), BF16),
            pltpu.VMEM((2 * EDGE, chans + chans // 2), BF16),
            pltpu.VMEM((2 * EDGE, chans + chans // 2), BF16),
            pltpu.VMEM((3 * tiles, rows + EDGE, LANES), F32),
            pltpu.VMEM((rows, chans), BF16),
            pltpu.VMEM((3, EDGE, chans), F32),
            pltpu.VMEM((tiles, 2 * LANES, LANES), BF16),
            pltpu.VMEM((tiles, LANES, LANES), F32),
            pltpu.VMEM((tiles, rows, per * LANES), BF16),
            pltpu.VMEM((rows, chans), F32),
            pltpu.VMEM((rows, chans), F32),
            pltpu.VMEM((modes, chans), F32),
            pltpu.VMEM((n, modes, chans), F32),
            pltpu.VMEM((wide, 2 * size), F32),
            pltpu.VMEM((wide, LANES), F32),
            pltpu.VMEM((rows, chans), BF16),
            pltpu.VMEM((wide, size), BF16),
            dma((4,)), dma((2,)), dma((n, 2)), dma((n, 2)),
            dma, dma, dma((n,)), dma((n,)),
        ],
        compiler_params=pltpu.CompilerParams(
            collective_id=0, has_side_effects=True, vmem_limit_bytes=40 * 1024 * 1024),
        name="mixers",
    )(
        jnp.transpose(streams, (1, 0, 2)),
        jnp.transpose(short_taps, (1, 0, 2)),
        modal_residue,
        modal_rate,
        skip_gain.reshape(1, chans),
        queries.reshape(wide, size),
        keys.reshape(rows, size),
        values.reshape(rows, size),
    )
    return hyena, attn.reshape(rows, heads, size)


def solution(mesh):
    in_specs = (
        P(("dp", "ctx"), None, "mp"),
        P(None, None, "mp"),
        P(None, "mp"),
        P(None, "mp"),
        P("mp"),
        P(("dp", "ctx"), "mp", None),
        P(("dp", "ctx"), "mp", None),
        P(("dp", "ctx"), "mp", None),
    )
    out_specs = (P(("dp", "ctx"), "mp"), P(("dp", "ctx"), "mp", None))
    return jax.shard_map(functools.partial(body, mesh.shape["ctx"]), mesh=mesh,
                         in_specs=in_specs, out_specs=out_specs, check_vma=False)
```

time: 133 us -> 23.3 us (0.18)
  the two profiles are of different devices: /device:TPU:0 before, /device:TPU:24 now
where the time goes in v1:
time: 23.3 us; the launch traced here: 22.9 us
  Pallas kernels  15.2 us (65%)
  local copies, waits for them, and re-layouts  7.01 us (30%)
  between operations  0.66 us (3%)
    pallas_call x1, Pallas kernels, body(): pl.pallas_call(functools.partial(kernel, n, heads, chunk), out_shape=(jax...  15.2 us
    unnamed x18, local copies, waits for them, and re-layouts  7.01 us

profile of v1, /device:TPU:24, one launch (start us, length us, event | category | flops | bytes accessed | tf_op | source)
XLA Modules:
  0.0 22.9 jit_solution(5044064505163010452)
XLA Ops:
  0.6 0.0 copy-start.7
  0.6 0.0 copy-start.4
  0.6 0.7 %copy-done.7 = f32[768]{0:T(1024)S(1)} copy-done((f32[768]{0:T(1024)S(1)}, f32[768]{0:T(1024)}, u32[]{:S(2)}) %copy-start.7) | copy-done | bytes 3096
  1.3 0.0 copy-done.4
  1.4 0.0 copy-start
  1.4 1.1 %copy-done = bf16[128,3,768]{2,0,1:T(8,128)(2,1)S(1)} copy-done((bf16[128,3,768]{2,0,1:T(8,128)(2,1)S(1)}, bf16[128,3,768]{2,0,1:T(8,128)(2,1)}, u32[]{:S(2)}) %copy-start) | copy-done | bytes 589848
  2.4 0.0 copy-start.1
  2.4 0.9 %copy-done.1 = bf16[128,8,128]{2,1,0:T(8,128)(2,1)S(1)} copy-done((bf16[128,8,128]{2,1,0:T(8,128)(2,1)S(1)}, bf16[128,8,128]{2,1,0:T(8,128)(2,1)}, u32[]{:S(2)}) %copy-start.1) | copy-done | bytes 262168
  3.4 0.0 copy-start.2
  3.4 0.8 %copy-done.2 = bf16[128,1,128]{2,0,1:T(8,128)(2,1)S(1)} copy-done((bf16[128,1,128]{2,0,1:T(8,128)(2,1)S(1)}, bf16[128,1,128]{2,0,1:T(8,128)(2,1)}, u32[]{:S(2)}) %copy-start.2) | copy-done | bytes 32792
  4.1 0.0 copy-start.3
  4.1 0.8 %copy-done.3 = bf16[128,1,128]{2,0,1:T(8,128)(2,1)S(1)} copy-done((bf16[128,1,128]{2,0,1:T(8,128)(2,1)S(1)}, bf16[128,1,128]{2,0,1:T(8,128)(2,1)}, u32[]{:S(2)}) %copy-start.3) | copy-done | bytes 32792
  4.9 0.0 copy-start.5
  4.9 0.7 %copy-done.5 = f32[16,48]{1,0:T(8,128)S(1)} copy-done((f32[16,48]{1,0:T(8,128)S(1)}, f32[16,48]{1,0:T(8,128)}, u32[]{:S(2)}) %copy-start.5) | copy-done | bytes 3096
  5.6 0.0 copy-start.6
  5.6 0.7 %copy-done.6 = f32[16,48]{1,0:T(8,128)S(1)} copy-done((f32[16,48]{1,0:T(8,128)S(1)}, f32[16,48]{1,0:T(8,128)}, u32[]{:S(2)}) %copy-start.6) | copy-done | bytes 3096
  6.3 15.2 %mixers.1 = (bf16[128,768]{1,0:T(8,128)(2,1)S(1)}, bf16[1024,128]{1,0:T(8,128)(2,1)S(1)}) custom-call(bf16[3,128,768]{2,1,0:T(8,128)(2,1)S(1)} %bitcast.6, f32[3,7,48]{2,1,0:T(8,128)S(1)} %bitcast.11, f32[16,48]{1,0:T(8,128)S(1)} %copy-done.5, f32[16,48]{1,0:T(8,128)S(1)} %copy-done.6, f32[1,768]{1,0:T(1,128)S(1)} %reshape.19.skip, ...), custom_call_target="tpu_custom_call" | custom-call | tf_op jit(solution)/shard_map/mixers/pallas_call | solution.py:281
  21.5 0.7 %copy.12 = bf16[128,768]{1,0:T(8,128)(2,1)} copy(bf16[128,768]{1,0:T(8,128)(2,1)S(1)} %get-tuple-element.8) | data formatting | bytes 393216
  22.2 0.7 %copy.13 = bf16[128,8,128]{2,1,0:T(8,128)(2,1)} copy(bf16[128,8,128]{2,1,0:T(8,128)(2,1)S(1)} %bitcast.8) | data formatting | bytes 524288
  (1 shorter events, 0.0 us)
Async XLA Ops:
  0.6 0.7 %copy-start.7 = (f32[768]{0:T(1024)S(1)}, f32[768]{0:T(1024)}, u32[]{:S(2)}) copy-start(f32[768]{0:T(1024)} %param.12) | copy-start | bytes 9220
  0.6 0.7 %copy-start.4 = (f32[7,3,48]{2,0,1:T(8,128)S(1)}, f32[7,3,48]{2,0,1:T(8,128)}, u32[]{:S(2)}) copy-start(f32[7,3,48]{2,0,1:T(8,128)} %param.9) | copy-start | bytes 12100
  1.4 1.1 %copy-start = (bf16[128,3,768]{2,0,1:T(8,128)(2,1)S(1)}, bf16[128,3,768]{2,0,1:T(8,128)(2,1)}, u32[]{:S(2)}) copy-start(bf16[128,3,768]{2,0,1:T(8,128)(2,1)} %param.8) | copy-start | bytes 1769476
  2.4 0.9 %copy-start.1 = (bf16[128,8,128]{2,1,0:T(8,128)(2,1)S(1)}, bf16[128,8,128]{2,1,0:T(8,128)(2,1)}, u32[]{:S(2)}) copy-start(bf16[128,8,128]{2,1,0:T(8,128)(2,1)} %param.13) | copy-start | bytes 786436
  3.4 0.8 %copy-start.2 = (bf16[128,1,128]{2,0,1:T(8,128)(2,1)S(1)}, bf16[128,1,128]{2,0,1:T(8,128)(2,1)}, u32[]{:S(2)}) copy-start(bf16[128,1,128]{2,0,1:T(8,128)(2,1)} %param.14) | copy-start | bytes 98308
  4.1 0.8 %copy-start.3 = (bf16[128,1,128]{2,0,1:T(8,128)(2,1)S(1)}, bf16[128,1,128]{2,0,1:T(8,128)(2,1)}, u32[]{:S(2)}) copy-start(bf16[128,1,128]{2,0,1:T(8,128)(2,1)} %param.15) | copy-start | bytes 98308
  4.9 0.7 %copy-start.5 = (f32[16,48]{1,0:T(8,128)S(1)}, f32[16,48]{1,0:T(8,128)}, u32[]{:S(2)}) copy-start(f32[16,48]{1,0:T(8,128)} %residue.1) | copy-start | bytes 9220
  5.6 0.7 %copy-start.6 = (f32[16,48]{1,0:T(8,128)S(1)}, f32[16,48]{1,0:T(8,128)}, u32[]{:S(2)}) copy-start(f32[16,48]{1,0:T(8,128)} %rate.1) | copy-start | bytes 9220

commit v2 on v1

--- a/solution.py
+++ b/solution.py
@@ -34,13 +34,19 @@
     return high, (value - high.astype(F32)).astype(BF16)
 
 
+def split_f32(value):
+    high = value.astype(BF16).astype(F32)
+    return high, value - high
+
+
 def kernel(
     n, heads, chunk,
-    streams, taps, residue, rate, skip, q_in, k_in, v_in,
-    hy_out, at_out,
-    xs, qv, kv, rim_tx, rim_rx, ext, gated, tapx, decay, coeff, toep, longt, gate,
-    st_tx, st_rx, acc, big, hy_v, at_v,
-    in_sem, out_sem, kv_send, kv_recv, rim_send, rim_recv, st_send, st_recv,
+    streams, taps_in, residue_in, rate_in, skip_in, q_in, k_in, v_in,
+    hy_v, at_v,
+    taps, residue, rate, skip,
+    xs, qv, kv, rim_tx, rim_rx, ext, gated, mixed, tapx, decay, coeff, toep, longt, gate,
+    st_tx, st_rx, acc, big,
+    in_sem, kv_send, kv_recv, rim_send, rim_recv, st_send, st_recv,
 ):
     me = lax.axis_index("ctx")
     rows, chans = xs.shape[1], xs.shape[2]
@@ -55,6 +61,10 @@
         pltpu.make_async_copy(k_in, kv.at[me, 0], in_sem.at[1]),
         pltpu.make_async_copy(v_in, kv.at[me, 1], in_sem.at[2]),
         pltpu.make_async_copy(q_in, qv, in_sem.at[3]),
+        pltpu.make_async_copy(rate_in, rate, in_sem.at[4]),
+        pltpu.make_async_copy(residue_in, residue, in_sem.at[5]),
+        pltpu.make_async_copy(taps_in, taps, in_sem.at[6]),
+        pltpu.make_async_copy(skip_in, skip, in_sem.at[7]),
     ]
     for copy in in_copies:
         copy.start()
@@ -107,12 +117,23 @@
             kv_copy(0, d).start()
             kv_copy(1, d).start()
 
+    for copy in in_copies[4:]:
+        copy.wait()
     spread = (iota((groups, chans), 1) // GSIZE == iota((groups, chans), 0)).astype(F32)
-    highest = lax.Precision.HIGHEST
+    spread = spread.astype(BF16)
+    mixed[...] = jnp.zeros(mixed.shape, F32)
     for j in range(3):
-        tapx[j, : reach + 1, :] = jnp.dot(
-            taps[j], spread, precision=highest, preferred_element_type=F32)
-    rate_nc = jnp.dot(rate[...], spread, precision=highest, preferred_element_type=F32)
+        mixed[EDGE * j:EDGE * j + reach + 1, :] = taps[j]
+    mixed[3 * EDGE:, :] = rate[...]
+    whole = mixed[...]
+    high, rest = split_f32(whole)
+    middle, rest = split_f32(rest)
+    count = 3 * EDGE + modes
+    spread_out = dot(jnp.concatenate([high, middle, rest], axis=0).astype(BF16), spread)
+    spread_out = (spread_out[2 * count:] + spread_out[count:2 * count]) + spread_out[:count]
+    for j in range(3):
+        tapx[j] = spread_out[EDGE * j:EDGE * (j + 1)]
+    rate_nc = spread_out[3 * EDGE:]
     step_decay = jnp.exp(rate_nc * (-float(rows)))
 
     for j in range(3):
@@ -184,57 +205,60 @@
         def _():
             st_copy(d).start()
 
-    pick_rows = iota((rows, LANES), 1) // GSIZE
+    picks = [(iota((1, LANES), 1) // GSIZE == gg).astype(F32).astype(BF16) for gg in range(per)]
     for q in range(tiles):
         cut = slice(q * LANES, (q + 1) * LANES)
         own = gated[:, cut]
-        parts = jnp.concatenate(
-            [jnp.where(pick_rows == gg, own, jnp.zeros_like(own)) for gg in range(per)], axis=0)
-        longt[:, cut] = dot(toep[q], parts) + skip[:, cut] * own.astype(F32)
+        parts = jnp.concatenate([own * picks[gg] for gg in range(per)], axis=0)
+        skip_row = skip[cut].reshape(1, LANES)
+        longt[:, cut] = dot(toep[q], parts) + skip_row * own.astype(F32)
         gate[:, cut] = filtered(0, q, 0, rows)
 
     scale = math.log2(math.e) / math.sqrt(LANES)
-    for copy in in_copies[1:]:
+    for copy in in_copies[1:4]:
         copy.wait()
-    ones = jnp.ones((rows, LANES), BF16)
+    ones = jnp.ones((HEAD_ROWS, rows), BF16)
     wide = heads * rows
-
-    own_value = jnp.concatenate([kv[me, 1], ones], axis=1)
-    own_key = kv[me, 0]
+    last = LANES + EDGE
+
+    def values_of(source):
+        turned = jnp.transpose(kv[source, 1].astype(F32)).astype(BF16)
+        return jnp.concatenate([turned, ones], axis=0)
+
+    own_value = values_of(me)
     for c in range(wide // chunk):
         cut = slice(c * chunk, (c + 1) * chunk)
-        scores = dot_nt(qv[cut, :], own_key) * scale
-        target = (iota((chunk, LANES), 0) + c * chunk) // heads
-        scores = jnp.where(iota((chunk, LANES), 1) <= target, scores, -1e30)
-        largest = jnp.broadcast_to(jnp.max(scores, axis=1, keepdims=True), (chunk, LANES))
-        weights = jnp.exp2(scores - largest).astype(BF16)
-        big[cut, :] = largest
-        acc[cut, :] = dot(weights, own_value)
+        seen = (c + 1) * chunk // heads
+        scores = dot_nt(kv[me, 0, :seen, :], qv[cut, :])
+        target = (iota((seen, chunk), 1) + c * chunk) // heads
+        scores = jnp.where(iota((seen, chunk), 0) <= target, scores, -1e30)
+        largest = jnp.max(scores, axis=0, keepdims=True)
+        weights = jnp.exp2((scores - largest) * scale).astype(BF16)
+        big[:, cut] = jnp.broadcast_to(largest, (EDGE, chunk))
+        acc[:, cut] = dot(own_value[:, :seen], weights)[:last]
 
     def far_block(d, carry):
         source = me - d
         kv_arrival(0, source).wait_recv()
         kv_arrival(1, source).wait_recv()
-        value = jnp.concatenate([kv[source, 1], ones], axis=1)
-        key = kv[source, 0]
+        value = values_of(source)
         for c in range(wide // chunk):
             cut = slice(c * chunk, (c + 1) * chunk)
-            scores = dot_nt(qv[cut, :], key) * scale
-            before = big[cut, :]
-            largest = jnp.maximum(before, jnp.max(scores, axis=1, keepdims=True))
-            weights = jnp.exp2(scores - largest).astype(BF16)
-            fix = jnp.exp2(before - largest)
-            big[cut, :] = largest
-            acc[cut, :] = acc[cut, :] * jnp.concatenate([fix, fix], axis=1) + dot(weights, value)
+            scores = dot_nt(kv[source, 0], qv[cut, :])
+            before = big[:1, cut]
+            largest = jnp.maximum(before, jnp.max(scores, axis=0, keepdims=True))
+            weights = jnp.exp2((scores - largest) * scale).astype(BF16)
+            fix = jnp.exp2((before - largest) * scale)
+            big[:, cut] = jnp.broadcast_to(largest, (EDGE, chunk))
+            acc[:, cut] = acc[:, cut] * fix + dot(value, weights)[:last]
         return carry
 
     lax.fori_loop(1, me + 1, far_block, 0)
 
-    for c in range(wide // chunk):
-        cut = slice(c * chunk, (c + 1) * chunk)
-        at_v[cut, :] = (acc[cut, :LANES] / acc[cut, LANES:]).astype(BF16)
-    at_copy = pltpu.make_async_copy(at_v, at_out, out_sem.at[0])
-    at_copy.start()
+    for c in range(wide // LANES):
+        cut = slice(c * LANES, (c + 1) * LANES)
+        ratio = acc[:LANES, cut] * (1.0 / acc[LANES:LANES + 1, cut])
+        at_v[cut, :] = jnp.transpose(ratio).astype(BF16)
 
     def gather_state(source, state):
         st_arrival(source).wait_recv()
@@ -250,8 +274,6 @@
         far = dot(jnp.concatenate([c_high, c_low, c_high], axis=1),
                   jnp.concatenate([s_high, s_high, s_low], axis=0))
         hy_v[:, cut] = (gate[:, cut] * (longt[:, cut] + far)).astype(BF16)
-    hy_copy = pltpu.make_async_copy(hy_v, hy_out, out_sem.at[1])
-    hy_copy.start()
 
     @pl.when(me < n - 1)
     def _():
@@ -263,8 +285,15 @@
             kv_copy(0, d).wait_send()
             kv_copy(1, d).wait_send()
             st_copy(d).wait_send()
-    at_copy.wait()
-    hy_copy.wait()
+
+
+def leave(hy_v, at_v, hy_out, at_out, sem):
+    copies = [pltpu.make_async_copy(hy_v, hy_out, sem.at[0]),
+              pltpu.make_async_copy(at_v, at_out, sem.at[1])]
+    for copy in copies:
+        copy.start()
+    for copy in copies:
+        copy.wait()
 
 
 def body(n, streams, short_taps, modal_residue, modal_rate, skip_gain, queries, keys, values):
@@ -276,15 +305,19 @@
     wide = heads * rows
     chunk = min(256, wide)
     reach = short_taps.shape[0]
-    vmem, hbm = pl.BlockSpec(memory_space=pltpu.VMEM), pl.BlockSpec(memory_space=pl.ANY)
+    vmem, hbm = pl.BlockSpec(memory_space=pltpu.VMEM), pl.BlockSpec(memory_space=pltpu.HBM)
     dma = pltpu.SemaphoreType.DMA
     hyena, attn = pl.pallas_call(
         functools.partial(kernel, n, heads, chunk),
         out_shape=(jax.ShapeDtypeStruct((rows, chans), BF16),
                    jax.ShapeDtypeStruct((wide, size), BF16)),
-        in_specs=[hbm, vmem, vmem, vmem, vmem, hbm, hbm, hbm],
-        out_specs=(hbm, hbm),
+        in_specs=[hbm] * 8,
+        out_specs=(vmem, vmem),
         scratch_shapes=[
+            pltpu.VMEM((3, reach, groups), F32),
+            pltpu.VMEM((modes, groups), F32),
+            pltpu.VMEM((modes, groups), F32),
+            pltpu.VMEM((chans,), F32),
             pltpu.VMEM((3, rows, chans), BF16),
             pltpu.VMEM((wide, size), BF16),
             pltpu.VMEM((n, 2, rows, size), BF16),
@@ -292,6 +325,7 @@
             pltpu.VMEM((2 * EDGE, chans + chans // 2), BF16),
             pltpu.VMEM((3 * tiles, rows + EDGE, LANES), F32),
             pltpu.VMEM((rows, chans), BF16),
+            pltpu.VMEM((3 * EDGE + modes, groups), F32),
             pltpu.VMEM((3, EDGE, chans), F32),
             pltpu.VMEM((tiles, 2 * LANES, LANES), BF16),
             pltpu.VMEM((tiles, LANES, LANES), F32),
@@ -300,26 +334,33 @@
             pltpu.VMEM((rows, chans), F32),
             pltpu.VMEM((modes, chans), F32),
             pltpu.VMEM((n, modes, chans), F32),
-            pltpu.VMEM((wide, 2 * size), F32),
-            pltpu.VMEM((wide, LANES), F32),
-            pltpu.VMEM((rows, chans), BF16),
-            pltpu.VMEM((wide, size), BF16),
-            dma((4,)), dma((2,)), dma((n, 2)), dma((n, 2)),
+            pltpu.VMEM((size + EDGE, wide), F32),
+            pltpu.VMEM((EDGE, wide), F32),
+            dma((8,)), dma((n, 2)), dma((n, 2)),
             dma, dma, dma((n,)), dma((n,)),
         ],
         compiler_params=pltpu.CompilerParams(
             collective_id=0, has_side_effects=True, vmem_limit_bytes=40 * 1024 * 1024),
         name="mixers",
-    )(
+    )(*[pltpu.with_memory_space_constraint(x, pltpu.HBM) for x in (
         jnp.transpose(streams, (1, 0, 2)),
         jnp.transpose(short_taps, (1, 0, 2)),
         modal_residue,
         modal_rate,
-        skip_gain.reshape(1, chans),
+        skip_gain,
         queries.reshape(wide, size),
         keys.reshape(rows, size),
         values.reshape(rows, size),
-    )
+    )])
+    hyena, attn = pl.pallas_call(
+        leave,
+        out_shape=(jax.ShapeDtypeStruct((rows, chans), BF16),
+                   jax.ShapeDtypeStruct((wide, size), BF16)),
+        in_specs=[vmem, vmem],
+        out_specs=(hbm, hbm),
+        scratch_shapes=[dma((2,))],
+        name="leave",
+    )(hyena, attn)
     return hyena, attn.reshape(rows, heads, size)
 
 

time: 23.3 us -> 18.7 us (0.80); the launches traced: 22.9 us -> 18.6 us
  local copies, waits for them, and re-layouts: 7.01 us -> 1.35 us
  Pallas kernels: 15.2 us -> 16.6 us
    unnamed x18 -> x4, local copies, waits for them, and re-layouts: 7.01 us -> 1.35 us
    pallas_call x0 -> x1, Pallas kernels: none -> 1.84 us  [body(): pl.pallas_call(leave, out_shape=(jax.ShapeDtypeStruct((rows, chans), BF16...]
    pallas_call x1, Pallas kernels: 15.2 us -> 14.7 us  [body(): pl.pallas_call(functools.partial(kernel, n, heads, chunk), out_shape=(jax...]
where the time goes in v2:
time: 18.7 us; the launch traced here: 18.6 us
  Pallas kernels  16.6 us (89%)
  local copies, waits for them, and re-layouts  1.35 us (7%)
  between operations  0.65 us (3%)
    pallas_call x1, Pallas kernels, body(): pl.pallas_call(functools.partial(kernel, n, heads, chunk), out_shape=(jax...  14.7 us
    pallas_call x1, Pallas kernels, body(): pl.pallas_call(leave, out_shape=(jax.ShapeDtypeStruct((rows, chans), BF16...  1.84 us
    unnamed x4, local copies, waits for them, and re-layouts  1.35 us

profile of v2, /device:TPU:24, one launch (start us, length us, event | category | flops | bytes accessed | tf_op | source)
XLA Modules:
  0.0 18.6 jit_solution(2154383815751639748)
XLA Ops:
  0.6 14.7 %mixers.1 = (bf16[128,768]{1,0:T(8,128)(2,1)S(1)}, bf16[1024,128]{1,0:T(8,128)(2,1)S(1)}) custom-call(bf16[3,128,768]{2,1,0:T(8,128)(2,1)} %bitcast.6, f32[3,7,48]{2,1,0:T(8,128)} %bitcast.10, f32[16,48]{1,0:T(8,128)} %residue_in.1, f32[16,48]{1,0:T(8,128)} %rate_in.1, f32[768]{0:T(1024)} %skip_in.1, bf16[1024,128]{1,0:T(8,128)(2,1)} %bitcast.7, ...), custom_call_target="tpu_custom_call" | custom-call | tf_op jit(solution)/shard_map/mixers/pallas_call | solution.py:310
  15.4 0.0 copy-start
  15.4 0.7 %copy-done = bf16[1024,128]{1,0:T(8,128)(2,1)} copy-done((bf16[1024,128]{1,0:T(8,128)(2,1)}, bf16[1024,128]{1,0:T(8,128)(2,1)S(1)}, u32[]{:S(2)}) %copy-start) | copy-done | bytes 262168
  16.0 0.0 copy-start.1
  16.1 0.7 %copy-done.1 = bf16[128,768]{1,0:T(8,128)(2,1)} copy-done((bf16[128,768]{1,0:T(8,128)(2,1)}, bf16[128,768]{1,0:T(8,128)(2,1)S(1)}, u32[]{:S(2)}) %copy-start.1) | copy-done | bytes 196632
  16.7 1.8 %leave.1 = (bf16[128,768]{1,0:T(8,128)(2,1)}, bf16[1024,128]{1,0:T(8,128)(2,1)}) custom-call(bf16[128,768]{1,0:T(8,128)(2,1)} %copy-done.1, bf16[1024,128]{1,0:T(8,128)(2,1)} %copy-done), custom_call_target="tpu_custom_call" | custom-call | tf_op jit(solution)/shard_map/leave/pallas_call | solution.py:355
Async XLA Ops:
  15.4 0.7 %copy-start = (bf16[1024,128]{1,0:T(8,128)(2,1)}, bf16[1024,128]{1,0:T(8,128)(2,1)S(1)}, u32[]{:S(2)}) copy-start(bf16[1024,128]{1,0:T(8,128)(2,1)S(1)} %get-tuple-element.7.at_v) | copy-start | bytes 786436
  16.0 0.7 %copy-start.1 = (bf16[128,768]{1,0:T(8,128)(2,1)}, bf16[128,768]{1,0:T(8,128)(2,1)S(1)}, u32[]{:S(2)}) copy-start(bf16[128,768]{1,0:T(8,128)(2,1)S(1)} %get-tuple-element.6.hy_v) | copy-start | bytes 589828

commit v3 on v2

--- a/solution.py
+++ b/solution.py
@@ -29,11 +29,6 @@
     return lax.dot_general(a, b, (((1,), (1,)), ((), ())), preferred_element_type=F32)
 
 
-def split_hi_lo(value):
-    high = value.astype(BF16)
-    return high, (value - high.astype(F32)).astype(BF16)
-
-
 def split_f32(value):
     high = value.astype(BF16).astype(F32)
     return high, value - high
@@ -44,7 +39,7 @@
     streams, taps_in, residue_in, rate_in, skip_in, q_in, k_in, v_in,
     hy_v, at_v,
     taps, residue, rate, skip,
-    xs, qv, kv, rim_tx, rim_rx, ext, gated, mixed, tapx, decay, coeff, toep, longt, gate,
+    xs, qv, kv, rim_tx, rim_rx, ext, gated, mixed, tapx, falls, decay, coeff, toep, longt, gate,
     st_tx, st_rx, acc, big,
     in_sem, kv_send, kv_recv, rim_send, rim_recv, st_send, st_recv,
 ):
@@ -75,15 +70,22 @@
         def _():
             pl.semaphore_signal(barrier, inc=1, device_id={"ctx": me - d}, device_id_type=MESH)
 
-    def kv_copy(part, d):
-        src = k_in if part == 0 else v_in
+    def kv_copy(part, source, d, own=False):
+        src = (k_in if part == 0 else v_in) if own else kv.at[source, part]
         return pltpu.make_async_remote_copy(
-            src_ref=src, dst_ref=kv.at[me, part], send_sem=kv_send.at[d, part],
-            recv_sem=kv_recv.at[me, part], device_id={"ctx": me + d}, device_id_type=MESH)
+            src_ref=src, dst_ref=kv.at[source, part], send_sem=kv_send.at[source, d - 1, part],
+            recv_sem=kv_recv.at[source, part], device_id={"ctx": me + d}, device_id_type=MESH)
+
+    def kv_each(source, own, act):
+        for d in (1, 2):
+            @pl.when(me + d < n)
+            def _():
+                act(kv_copy(0, source, d, own))
+                act(kv_copy(1, source, d, own))
 
     def kv_arrival(part, source):
         return pltpu.make_async_remote_copy(
-            src_ref=kv.at[source, part], dst_ref=kv.at[source, part], send_sem=kv_send.at[0, part],
+            src_ref=kv.at[source, part], dst_ref=kv.at[source, part], send_sem=kv_send.at[source, 0, part],
             recv_sem=kv_recv.at[source, part], device_id={"ctx": source}, device_id_type=MESH)
 
     def st_copy(d):
@@ -111,11 +113,7 @@
         pl.semaphore_wait(barrier, n - 1 - me)
         rim_copy().start()
 
-    for d in range(1, n):
-        @pl.when(me + d < n)
-        def _():
-            kv_copy(0, d).start()
-            kv_copy(1, d).start()
+    kv_each(me, True, lambda copy: copy.start())
 
     for copy in in_copies[4:]:
         copy.wait()
@@ -156,21 +154,13 @@
     fill_gated(HEAD_ROWS, rows)
 
     lane = iota((modes, LANES), 1).astype(F32)
-    causal = iota((rows, LANES), 1) <= iota((rows, LANES), 0)
     rate_v = rate[...]
-    residue_v = residue[...]
     for g in range(groups):
         rate_b = jnp.broadcast_to(rate_v[:, g:g + 1], (modes, LANES))
-        residue_b = jnp.broadcast_to(residue_v[:, g:g + 1], (modes, LANES))
         fall = jnp.exp(rate_b * (lane - (rows - 1.0)))
-        high, low = split_hi_lo(fall)
         q, gg = g // per, g % per
-        decay[q, gg * modes:(gg + 1) * modes, :] = high
-        decay[q, LANES + gg * modes:LANES + (gg + 1) * modes, :] = low
-        coeff[q, gg * modes:(gg + 1) * modes, :] = residue_b * jnp.exp(rate_b * (-1.0 - lane))
-        table = jnp.sum(residue_b * fall, axis=0, keepdims=True)
-        rolled = pltpu.roll(jnp.broadcast_to(table, (rows, LANES)), 1, 1, stride=1, stride_axis=0)
-        toep[q, :, gg * LANES:(gg + 1) * LANES] = jnp.where(causal, rolled, 0.0).astype(BF16)
+        falls[q, gg * modes:(gg + 1) * modes, :] = fall
+        decay[q, gg * modes:(gg + 1) * modes, :] = fall.astype(BF16)
 
     @pl.when(me > 0)
     def _():
@@ -195,15 +185,29 @@
         full = dot(decay[q], gated[:, cut])
         state = jnp.zeros((modes, LANES), F32)
         for gg in range(per):
-            both = (full[gg * modes:(gg + 1) * modes]
-                    + full[LANES + gg * modes:LANES + (gg + 1) * modes])
-            state = jnp.where(pick == gg, both, state)
-        st_tx[:, cut] = state
+            state = jnp.where(pick == gg, full[gg * modes:(gg + 1) * modes], state)
+        st_tx[:, cut] = state.astype(BF16)
 
     for d in range(1, n):
         @pl.when(me + d < n)
         def _():
             st_copy(d).start()
+
+    causal = iota((rows, LANES), 1) <= iota((rows, LANES), 0)
+    residue_v = residue[...]
+    for q in range(tiles):
+        turned = []
+        for gg in range(per):
+            g = q * per + gg
+            rate_b = jnp.broadcast_to(rate_v[:, g:g + 1], (modes, LANES))
+            residue_b = jnp.broadcast_to(residue_v[:, g:g + 1], (modes, LANES))
+            turned.append(residue_b * jnp.exp(rate_b * (-1.0 - lane)))
+            fall = falls[q, gg * modes:(gg + 1) * modes, :]
+            table = jnp.sum(residue_b * fall, axis=0, keepdims=True)
+            rolled = pltpu.roll(
+                jnp.broadcast_to(table, (rows, LANES)), 1, 1, stride=1, stride_axis=0)
+            toep[q, :, gg * LANES:(gg + 1) * LANES] = jnp.where(causal, rolled, 0.0).astype(BF16)
+        coeff[q] = jnp.transpose(jnp.concatenate(turned, axis=0)).astype(BF16)
 
     picks = [(iota((1, LANES), 1) // GSIZE == gg).astype(F32).astype(BF16) for gg in range(per)]
     for q in range(tiles):
@@ -224,6 +228,17 @@
     def values_of(source):
         turned = jnp.transpose(kv[source, 1].astype(F32)).astype(BF16)
         return jnp.concatenate([turned, ones], axis=0)
+
+    def forward(k, carry):
+        source = me - 2 * k
+        kv_arrival(0, source).wait_recv()
+        kv_arrival(1, source).wait_recv()
+        kv_each(source, False, lambda copy: copy.start())
+        return carry
+
+    @pl.when(me < n - 1)
+    def _():
+        lax.fori_loop(1, me // 2 + 1, forward, 0)
 
     own_value = values_of(me)
     for c in range(wide // chunk):
@@ -239,8 +254,12 @@
 
     def far_block(d, carry):
         source = me - d
-        kv_arrival(0, source).wait_recv()
-        kv_arrival(1, source).wait_recv()
+
+        @pl.when((lax.rem(d, 2) == 1) | (me == n - 1))
+        def _():
+            kv_arrival(0, source).wait_recv()
+            kv_arrival(1, source).wait_recv()
+
         value = values_of(source)
         for c in range(wide // chunk):
             cut = slice(c * chunk, (c + 1) * chunk)
@@ -262,17 +281,14 @@
 
     def gather_state(source, state):
         st_arrival(source).wait_recv()
-        return state * step_decay + st_rx[source]
+        return state * step_decay + st_rx[source].astype(F32)
 
     state = lax.fori_loop(0, me, gather_state, jnp.zeros((modes, chans), F32))
     for q in range(tiles):
         cut = slice(q * LANES, (q + 1) * LANES)
         block = jnp.concatenate(
             [jnp.where(pick == gg, state[:, cut], 0.0) for gg in range(per)], axis=0)
-        s_high, s_low = split_hi_lo(block)
-        c_high, c_low = split_hi_lo(jnp.transpose(coeff[q]))
-        far = dot(jnp.concatenate([c_high, c_low, c_high], axis=1),
-                  jnp.concatenate([s_high, s_high, s_low], axis=0))
+        far = dot(coeff[q], block.astype(BF16))
         hy_v[:, cut] = (gate[:, cut] * (longt[:, cut] + far)).astype(BF16)
 
     @pl.when(me < n - 1)
@@ -282,9 +298,15 @@
     for d in range(1, n):
         @pl.when(me + d < n)
         def _():
-            kv_copy(0, d).wait_send()
-            kv_copy(1, d).wait_send()
             st_copy(d).wait_send()
+
+    kv_each(me, True, lambda copy: copy.wait_send())
+
+    def forwarded(k, carry):
+        kv_each(me - 2 * k, False, lambda copy: copy.wait_send())
+        return carry
+
+    lax.fori_loop(1, me // 2 + 1, forwarded, 0)
 
 
 def leave(hy_v, at_v, hy_out, at_out, sem):
@@ -327,16 +349,17 @@
             pltpu.VMEM((rows, chans), BF16),
             pltpu.VMEM((3 * EDGE + modes, groups), F32),
             pltpu.VMEM((3, EDGE, chans), F32),
-            pltpu.VMEM((tiles, 2 * LANES, LANES), BF16),
             pltpu.VMEM((tiles, LANES, LANES), F32),
+            pltpu.VMEM((tiles, LANES, LANES), BF16),
+            pltpu.VMEM((tiles, LANES, LANES), BF16),
             pltpu.VMEM((tiles, rows, per * LANES), BF16),
             pltpu.VMEM((rows, chans), F32),
             pltpu.VMEM((rows, chans), F32),
-            pltpu.VMEM((modes, chans), F32),
-            pltpu.VMEM((n, modes, chans), F32),
+            pltpu.VMEM((modes, chans), BF16),
+            pltpu.VMEM((n, modes, chans), BF16),
             pltpu.VMEM((size + EDGE, wide), F32),
             pltpu.VMEM((EDGE, wide), F32),
-            dma((8,)), dma((n, 2)), dma((n, 2)),
+            dma((8,)), dma((n, 2, 2)), dma((n, 2)),
             dma, dma, dma((n,)), dma((n,)),
         ],
         compiler_params=pltpu.CompilerParams(
@@ -359,6 +382,7 @@
         in_specs=[vmem, vmem],
         out_specs=(hbm, hbm),
         scratch_shapes=[dma((2,))],
+        compiler_params=pltpu.CompilerParams(vmem_limit_bytes=2 * 1024 * 1024),
         name="leave",
     )(hyena, attn)
     return hyena, attn.reshape(rows, heads, size)

time: 18.7 us -> 14.8 us (0.79)
  Pallas kernels: 16.6 us -> 14 us
  local copies, waits for them, and re-layouts: 1.35 us -> 0 us
    pallas_call x1, Pallas kernels: 14.7 us -> 13.3 us  [body(): pl.pallas_call(functools.partial(kernel, n, heads, chunk), out_shape=(jax...]
    unnamed x4 -> x0, local copies, waits for them, and re-layouts: 1.35 us -> none
    pallas_call x1, Pallas kernels: 1.84 us -> 0.79 us  [body(): pl.pallas_call(leave, out_shape=(jax.ShapeDtypeStruct((rows, chans), BF16...]
where the time goes in v3:
time: 14.8 us; the launch traced here: 14.7 us
  Pallas kernels  14 us (95%)
  between operations  0.64 us (4%)
    pallas_call x1, Pallas kernels, body(): pl.pallas_call(functools.partial(kernel, n, heads, chunk), out_shape=(jax...  13.3 us
    pallas_call x1, Pallas kernels, body(): pl.pallas_call(leave, out_shape=(jax.ShapeDtypeStruct((rows, chans), BF16...  0.79 us

profile of v3, /device:TPU:24, one launch (start us, length us, event | category | flops | bytes accessed | tf_op | source)
XLA Modules:
  0.0 14.7 jit_solution(2655266177627710134)
XLA Ops:
  0.6 13.3 %mixers.1 = (bf16[128,768]{1,0:T(8,128)(2,1)S(1)}, bf16[1024,128]{1,0:T(8,128)(2,1)S(1)}) custom-call(bf16[3,128,768]{2,1,0:T(8,128)(2,1)} %bitcast.6, f32[3,7,48]{2,1,0:T(8,128)} %bitcast.10, f32[16,48]{1,0:T(8,128)} %residue_in.1, f32[16,48]{1,0:T(8,128)} %rate_in.1, f32[768]{0:T(1024)} %skip_in.1, bf16[1024,128]{1,0:T(8,128)(2,1)} %bitcast.7, ...), custom_call_target="tpu_custom_call" | custom-call | tf_op jit(solution)/shard_map/mixers/pallas_call | solution.py:332
  13.9 0.8 %leave.1 = (bf16[128,768]{1,0:T(8,128)(2,1)}, bf16[1024,128]{1,0:T(8,128)(2,1)}) custom-call(bf16[128,768]{1,0:T(8,128)(2,1)S(1)} %get-tuple-element.6.hy_v, bf16[1024,128]{1,0:T(8,128)(2,1)S(1)} %get-tuple-element.7.at_v), custom_call_target="tpu_custom_call" | custom-call | tf_op jit(solution)/shard_map/leave/pallas_call | solution.py:378

commit v4 on v3

--- a/solution.py
+++ b/solution.py
@@ -77,7 +77,7 @@
             recv_sem=kv_recv.at[source, part], device_id={"ctx": me + d}, device_id_type=MESH)
 
     def kv_each(source, own, act):
-        for d in (1, 2):
+        for d in (2, 1):
             @pl.when(me + d < n)
             def _():
                 act(kv_copy(0, source, d, own))
@@ -193,7 +193,8 @@
         def _():
             st_copy(d).start()
 
-    causal = iota((rows, LANES), 1) <= iota((rows, LANES), 0)
+    half_rows = rows // 2
+    causal = iota((half_rows, LANES), 1) <= iota((half_rows, LANES), 0) + half_rows
     residue_v = residue[...]
     for q in range(tiles):
         turned = []
@@ -205,17 +206,34 @@
             fall = falls[q, gg * modes:(gg + 1) * modes, :]
             table = jnp.sum(residue_b * fall, axis=0, keepdims=True)
             rolled = pltpu.roll(
-                jnp.broadcast_to(table, (rows, LANES)), 1, 1, stride=1, stride_axis=0)
+                jnp.broadcast_to(table, (half_rows, LANES)), half_rows + 1, 1,
+                stride=1, stride_axis=0)
             toep[q, :, gg * LANES:(gg + 1) * LANES] = jnp.where(causal, rolled, 0.0).astype(BF16)
         coeff[q] = jnp.transpose(jnp.concatenate(turned, axis=0)).astype(BF16)
 
-    picks = [(iota((1, LANES), 1) // GSIZE == gg).astype(F32).astype(BF16) for gg in range(per)]
+    def forward(k, carry):
+        source = me - 2 * k
+        kv_arrival(0, source).wait_recv()
+        kv_arrival(1, source).wait_recv()
+        kv_each(source, False, lambda copy: copy.start())
+        return carry
+
+    @pl.when(me < n - 1)
+    def _():
+        lax.fori_loop(1, me // 2 + 1, forward, 0)
+
+    picks = [(iota((1, 2 * LANES), 1) % LANES // GSIZE == gg).astype(F32).astype(BF16)
+             for gg in range(per)]
+    blank = jnp.zeros((half_rows, LANES), BF16)
     for q in range(tiles):
         cut = slice(q * LANES, (q + 1) * LANES)
         own = gated[:, cut]
-        parts = jnp.concatenate([own * picks[gg] for gg in range(per)], axis=0)
-        skip_row = skip[cut].reshape(1, LANES)
-        longt[:, cut] = dot(toep[q], parts) + skip_row * own.astype(F32)
+        moved = jnp.concatenate([blank, own[:half_rows]], axis=0)
+        pair = jnp.concatenate([moved, own], axis=1)
+        parts = jnp.concatenate([pair * picks[gg] for gg in range(per)], axis=0)
+        near = dot(toep[q], parts)
+        near = jnp.concatenate([near[:, :LANES], near[:, LANES:]], axis=0)
+        longt[:, cut] = near + skip[cut].reshape(1, LANES) * own.astype(F32)
         gate[:, cut] = filtered(0, q, 0, rows)
 
     scale = math.log2(math.e) / math.sqrt(LANES)
@@ -228,17 +246,6 @@
     def values_of(source):
         turned = jnp.transpose(kv[source, 1].astype(F32)).astype(BF16)
         return jnp.concatenate([turned, ones], axis=0)
-
-    def forward(k, carry):
-        source = me - 2 * k
-        kv_arrival(0, source).wait_recv()
-        kv_arrival(1, source).wait_recv()
-        kv_each(source, False, lambda copy: copy.start())
-        return carry
-
-    @pl.when(me < n - 1)
-    def _():
-        lax.fori_loop(1, me // 2 + 1, forward, 0)
 
     own_value = values_of(me)
     for c in range(wide // chunk):
@@ -272,12 +279,8 @@
             acc[:, cut] = acc[:, cut] * fix + dot(value, weights)[:last]
         return carry
 
-    lax.fori_loop(1, me + 1, far_block, 0)
-
-    for c in range(wide // LANES):
-        cut = slice(c * LANES, (c + 1) * LANES)
-        ratio = acc[:LANES, cut] * (1.0 / acc[LANES:LANES + 1, cut])
-        at_v[cut, :] = jnp.transpose(ratio).astype(BF16)
+    middle_block = jnp.maximum(me, jnp.minimum(me + 1, 2))
+    lax.fori_loop(1, middle_block, far_block, 0)
 
     def gather_state(source, state):
         st_arrival(source).wait_recv()
@@ -290,6 +293,13 @@
             [jnp.where(pick == gg, state[:, cut], 0.0) for gg in range(per)], axis=0)
         far = dot(coeff[q], block.astype(BF16))
         hy_v[:, cut] = (gate[:, cut] * (longt[:, cut] + far)).astype(BF16)
+
+    lax.fori_loop(middle_block, me + 1, far_block, 0)
+
+    for c in range(wide // LANES):
+        cut = slice(c * LANES, (c + 1) * LANES)
+        ratio = acc[:LANES, cut] * (1.0 / acc[LANES:LANES + 1, cut])
+        at_v[cut, :] = jnp.transpose(ratio).astype(BF16)
 
     @pl.when(me < n - 1)
     def _():
@@ -352,7 +362,7 @@
             pltpu.VMEM((tiles, LANES, LANES), F32),
             pltpu.VMEM((tiles, LANES, LANES), BF16),
             pltpu.VMEM((tiles, LANES, LANES), BF16),
-            pltpu.VMEM((tiles, rows, per * LANES), BF16),
+            pltpu.VMEM((tiles, rows // 2, per * LANES), BF16),
             pltpu.VMEM((rows, chans), F32),
             pltpu.VMEM((rows, chans), F32),
             pltpu.VMEM((modes, chans), BF16),

time: 14.8 us -> 14.2 us (0.959)
  Pallas kernels: 14 us -> 13.4 us
    pallas_call x1, Pallas kernels: 13.3 us -> 12.6 us  [body(): pl.pallas_call(functools.partial(kernel, n, heads, chunk), out_shape=(jax...]
where the time goes in v4:
time: 14.2 us; the launch traced here: 14 us
  Pallas kernels  13.4 us (94%)
  between operations  0.64 us (5%)
    pallas_call x1, Pallas kernels, body(): pl.pallas_call(functools.partial(kernel, n, heads, chunk), out_shape=(jax...  12.6 us
    pallas_call x1, Pallas kernels, body(): pl.pallas_call(leave, out_shape=(jax.ShapeDtypeStruct((rows, chans), BF16...  0.79 us

profile of v4, /device:TPU:24, one launch (start us, length us, event | category | flops | bytes accessed | tf_op | source)
XLA Modules:
  0.0 14.0 jit_solution(18312443678383943113)
XLA Ops:
  0.6 12.6 %mixers.1 = (bf16[128,768]{1,0:T(8,128)(2,1)S(1)}, bf16[1024,128]{1,0:T(8,128)(2,1)S(1)}) custom-call(bf16[3,128,768]{2,1,0:T(8,128)(2,1)} %bitcast.6, f32[3,7,48]{2,1,0:T(8,128)} %bitcast.10, f32[16,48]{1,0:T(8,128)} %residue_in.1, f32[16,48]{1,0:T(8,128)} %rate_in.1, f32[768]{0:T(1024)} %skip_in.1, bf16[1024,128]{1,0:T(8,128)(2,1)} %bitcast.7, ...), custom_call_target="tpu_custom_call" | custom-call | tf_op jit(solution)/shard_map/mixers/pallas_call | solution.py:342
  13.2 0.8 %leave.1 = (bf16[128,768]{1,0:T(8,128)(2,1)}, bf16[1024,128]{1,0:T(8,128)(2,1)}) custom-call(bf16[128,768]{1,0:T(8,128)(2,1)S(1)} %get-tuple-element.6.hy_v, bf16[1024,128]{1,0:T(8,128)(2,1)S(1)} %get-tuple-element.7.at_v), custom_call_target="tpu_custom_call" | custom-call | tf_op jit(solution)/shard_map/leave/pallas_call | solution.py:388

commit v5 on v4

--- a/solution.py
+++ b/solution.py
@@ -40,7 +40,7 @@
     hy_v, at_v,
     taps, residue, rate, skip,
     xs, qv, kv, rim_tx, rim_rx, ext, gated, mixed, tapx, falls, decay, coeff, toep, longt, gate,
-    st_tx, st_rx, acc, big,
+    st_tx, st_rx, run_p, run_e, acc, big, fixes, wts,
     in_sem, kv_send, kv_recv, rim_send, rim_recv, st_send, st_recv,
 ):
     me = lax.axis_index("ctx")
@@ -76,27 +76,42 @@
             src_ref=src, dst_ref=kv.at[source, part], send_sem=kv_send.at[source, d - 1, part],
             recv_sem=kv_recv.at[source, part], device_id={"ctx": me + d}, device_id_type=MESH)
 
-    def kv_each(source, own, act):
+    def kv_each(source, own, act, parts=(0, 1)):
         for d in (2, 1):
             @pl.when(me + d < n)
             def _():
-                act(kv_copy(0, source, d, own))
-                act(kv_copy(1, source, d, own))
+                for part in parts:
+                    act(kv_copy(part, source, d, own))
 
     def kv_arrival(part, source):
         return pltpu.make_async_remote_copy(
             src_ref=kv.at[source, part], dst_ref=kv.at[source, part], send_sem=kv_send.at[source, 0, part],
             recv_sem=kv_recv.at[source, part], device_id={"ctx": source}, device_id_type=MESH)
 
-    def st_copy(d):
+    steps = (n - 1).bit_length()
+
+    def st_copy(k):
         return pltpu.make_async_remote_copy(
-            src_ref=st_tx, dst_ref=st_rx.at[me], send_sem=st_send.at[d],
-            recv_sem=st_recv.at[me], device_id={"ctx": me + d}, device_id_type=MESH)
-
-    def st_arrival(source):
-        return pltpu.make_async_remote_copy(
-            src_ref=st_tx, dst_ref=st_rx.at[source], send_sem=st_send.at[0],
-            recv_sem=st_recv.at[source], device_id={"ctx": source}, device_id_type=MESH)
+            src_ref=st_tx.at[k], dst_ref=st_rx.at[k], send_sem=st_send.at[k],
+            recv_sem=st_recv.at[k], device_id={"ctx": lax.rem(me + 2 ** k, n)},
+            device_id_type=MESH)
+
+    def st_out(k):
+        st_tx[k] = run_p[...].astype(BF16)
+
+        @pl.when(me + 2 ** k < n)
+        def _():
+            st_copy(k).start()
+
+    def st_in(k):
+        @pl.when(me >= 2 ** k)
+        def _():
+            st_copy(k).wait_recv()
+            got = st_rx[k].astype(F32)
+            fall = -float(rows) * rate_nc
+            run_e[...] += got if k == 0 else got * jnp.exp(fall * (2 ** k - 1.0))
+            if k + 1 < steps:
+                run_p[...] += got * jnp.exp(fall * float(2 ** k))
 
     def rim_copy():
         return pltpu.make_async_remote_copy(
@@ -132,7 +147,6 @@
     for j in range(3):
         tapx[j] = spread_out[EDGE * j:EDGE * (j + 1)]
     rate_nc = spread_out[3 * EDGE:]
-    step_decay = jnp.exp(rate_nc * (-float(rows)))
 
     for j in range(3):
         for q in range(tiles):
@@ -186,12 +200,9 @@
         state = jnp.zeros((modes, LANES), F32)
         for gg in range(per):
             state = jnp.where(pick == gg, full[gg * modes:(gg + 1) * modes], state)
-        st_tx[:, cut] = state.astype(BF16)
-
-    for d in range(1, n):
-        @pl.when(me + d < n)
-        def _():
-            st_copy(d).start()
+        run_p[:, cut] = state
+    run_e[...] = jnp.zeros(run_e.shape, F32)
+    st_out(0)
 
     half_rows = rows // 2
     causal = iota((half_rows, LANES), 1) <= iota((half_rows, LANES), 0) + half_rows
@@ -213,9 +224,9 @@
 
     def forward(k, carry):
         source = me - 2 * k
-        kv_arrival(0, source).wait_recv()
-        kv_arrival(1, source).wait_recv()
-        kv_each(source, False, lambda copy: copy.start())
+        for part in range(2):
+            kv_arrival(part, source).wait_recv()
+            kv_each(source, False, lambda copy: copy.start(), (part,))
         return carry
 
     @pl.when(me < n - 1)
@@ -236,6 +247,10 @@
         longt[:, cut] = near + skip[cut].reshape(1, LANES) * own.astype(F32)
         gate[:, cut] = filtered(0, q, 0, rows)
 
+    for k in range(steps - 1):
+        st_in(k)
+        st_out(k + 1)
+
     scale = math.log2(math.e) / math.sqrt(LANES)
     for copy in in_copies[1:4]:
         copy.wait()
@@ -259,56 +274,72 @@
         big[:, cut] = jnp.broadcast_to(largest, (EDGE, chunk))
         acc[:, cut] = dot(own_value[:, :seen], weights)[:last]
 
-    def far_block(d, carry):
-        source = me - d
-
-        @pl.when((lax.rem(d, 2) == 1) | (me == n - 1))
+    def weigh(source, waits):
+        @pl.when(waits)
         def _():
             kv_arrival(0, source).wait_recv()
-            kv_arrival(1, source).wait_recv()
-
-        value = values_of(source)
+
         for c in range(wide // chunk):
             cut = slice(c * chunk, (c + 1) * chunk)
             scores = dot_nt(kv[source, 0], qv[cut, :])
             before = big[:1, cut]
             largest = jnp.maximum(before, jnp.max(scores, axis=0, keepdims=True))
-            weights = jnp.exp2((scores - largest) * scale).astype(BF16)
+            wts[:, cut] = jnp.exp2((scores - largest) * scale).astype(BF16)
             fix = jnp.exp2((before - largest) * scale)
             big[:, cut] = jnp.broadcast_to(largest, (EDGE, chunk))
-            acc[:, cut] = acc[:, cut] * fix + dot(value, weights)[:last]
+            fixes[:, cut] = jnp.broadcast_to(fix, (EDGE, chunk))
+
+        @pl.when(waits)
+        def _():
+            kv_arrival(1, source).wait_recv()
+
+    def finish(c, total):
+        for part in range(chunk // LANES):
+            cut = slice(part * LANES, (part + 1) * LANES)
+            ratio = total[:LANES, cut] * (1.0 / total[LANES:LANES + 1, cut])
+            low = c * chunk + part * LANES
+            at_v[low:low + LANES, :] = jnp.transpose(ratio).astype(BF16)
+
+    def far_block(d, carry):
+        source = me - d
+        weigh(source, (lax.rem(d, 2) == 1) | (me == n - 1))
+        value = values_of(source)
+        for c in range(wide // chunk):
+            cut = slice(c * chunk, (c + 1) * chunk)
+            acc[:, cut] = acc[:, cut] * fixes[:1, cut] + dot(value, wts[:, cut])[:last]
         return carry
 
-    middle_block = jnp.maximum(me, jnp.minimum(me + 1, 2))
-    lax.fori_loop(1, middle_block, far_block, 0)
-
-    def gather_state(source, state):
-        st_arrival(source).wait_recv()
-        return state * step_decay + st_rx[source].astype(F32)
-
-    state = lax.fori_loop(0, me, gather_state, jnp.zeros((modes, chans), F32))
+    lax.fori_loop(1, me, far_block, 0)
+
+    st_in(steps - 1)
     for q in range(tiles):
         cut = slice(q * LANES, (q + 1) * LANES)
         block = jnp.concatenate(
-            [jnp.where(pick == gg, state[:, cut], 0.0) for gg in range(per)], axis=0)
+            [jnp.where(pick == gg, run_e[:, cut], 0.0) for gg in range(per)], axis=0)
         far = dot(coeff[q], block.astype(BF16))
         hy_v[:, cut] = (gate[:, cut] * (longt[:, cut] + far)).astype(BF16)
 
-    lax.fori_loop(middle_block, me + 1, far_block, 0)
-
-    for c in range(wide // LANES):
-        cut = slice(c * LANES, (c + 1) * LANES)
-        ratio = acc[:LANES, cut] * (1.0 / acc[LANES:LANES + 1, cut])
-        at_v[cut, :] = jnp.transpose(ratio).astype(BF16)
+    @pl.when(me > 0)
+    def _():
+        weigh(0, (lax.rem(me, 2) == 1) | (me == n - 1))
+        value = values_of(0)
+        for c in range(wide // chunk):
+            cut = slice(c * chunk, (c + 1) * chunk)
+            finish(c, acc[:, cut] * fixes[:1, cut] + dot(value, wts[:, cut])[:last])
+
+    @pl.when(me == 0)
+    def _():
+        for c in range(wide // chunk):
+            finish(c, acc[:, c * chunk:(c + 1) * chunk])
 
     @pl.when(me < n - 1)
     def _():
         rim_copy().wait_send()
 
-    for d in range(1, n):
-        @pl.when(me + d < n)
-        def _():
-            st_copy(d).wait_send()
+    for k in range(steps):
+        @pl.when(me + 2 ** k < n)
+        def _():
+            st_copy(k).wait_send()
 
     kv_each(me, True, lambda copy: copy.wait_send())
 
@@ -337,6 +368,7 @@
     wide = heads * rows
     chunk = min(256, wide)
     reach = short_taps.shape[0]
+    steps = (n - 1).bit_length()
     vmem, hbm = pl.BlockSpec(memory_space=pltpu.VMEM), pl.BlockSpec(memory_space=pltpu.HBM)
     dma = pltpu.SemaphoreType.DMA
     hyena, attn = pl.pallas_call(
@@ -365,12 +397,16 @@
             pltpu.VMEM((tiles, rows // 2, per * LANES), BF16),
             pltpu.VMEM((rows, chans), F32),
             pltpu.VMEM((rows, chans), F32),
-            pltpu.VMEM((modes, chans), BF16),
-            pltpu.VMEM((n, modes, chans), BF16),
+            pltpu.VMEM((steps, modes, chans), BF16),
+            pltpu.VMEM((steps, modes, chans), BF16),
+            pltpu.VMEM((modes, chans), F32),
+            pltpu.VMEM((modes, chans), F32),
             pltpu.VMEM((size + EDGE, wide), F32),
             pltpu.VMEM((EDGE, wide), F32),
+            pltpu.VMEM((EDGE, wide), F32),
+            pltpu.VMEM((rows, wide), BF16),
             dma((8,)), dma((n, 2, 2)), dma((n, 2)),
-            dma, dma, dma((n,)), dma((n,)),
+            dma, dma, dma((steps,)), dma((steps,)),
         ],
         compiler_params=pltpu.CompilerParams(
             collective_id=0, has_side_effects=True, vmem_limit_bytes=40 * 1024 * 1024),

time: 14.2 us -> 14.9 us (1.049)
  Pallas kernels: 13.4 us -> 14.1 us
    pallas_call x1, Pallas kernels: 12.6 us -> 13.3 us  [body(): pl.pallas_call(functools.partial(kernel, n, heads, chunk), out_shape=(jax...]
where the time goes in v5:
time: 14.9 us; the launch traced here: 14.7 us
  Pallas kernels  14.1 us (95%)
  between operations  0.64 us (4%)
    pallas_call x1, Pallas kernels, body(): pl.pallas_call(functools.partial(kernel, n, heads, chunk), out_shape=(jax...  13.3 us
    pallas_call x1, Pallas kernels, body(): pl.pallas_call(leave, out_shape=(jax.ShapeDtypeStruct((rows, chans), BF16...  0.79 us

profile of v5, /device:TPU:24, one launch (start us, length us, event | category | flops | bytes accessed | tf_op | source)
XLA Modules:
  0.0 14.7 jit_solution(6026015892397714248)
XLA Ops:
  0.6 13.3 %mixers.1 = (bf16[128,768]{1,0:T(8,128)(2,1)S(1)}, bf16[1024,128]{1,0:T(8,128)(2,1)S(1)}) custom-call(bf16[3,128,768]{2,1,0:T(8,128)(2,1)} %bitcast.6, f32[3,7,48]{2,1,0:T(8,128)} %bitcast.10, f32[16,48]{1,0:T(8,128)} %residue_in.1, f32[16,48]{1,0:T(8,128)} %rate_in.1, f32[768]{0:T(1024)} %skip_in.1, bf16[1024,128]{1,0:T(8,128)(2,1)} %bitcast.7, ...), custom_call_target="tpu_custom_call" | custom-call | tf_op jit(solution)/shard_map/mixers/pallas_call | solution.py:374
  13.9 0.8 %leave.1 = (bf16[128,768]{1,0:T(8,128)(2,1)}, bf16[1024,128]{1,0:T(8,128)(2,1)}) custom-call(bf16[128,768]{1,0:T(8,128)(2,1)S(1)} %get-tuple-element.6.hy_v, bf16[1024,128]{1,0:T(8,128)(2,1)S(1)} %get-tuple-element.7.at_v), custom_call_target="tpu_custom_call" | custom-call | tf_op jit(solution)/shard_map/leave/pallas_call | solution.py:424

commit v6 on v4

--- a/solution.py
+++ b/solution.py
@@ -39,7 +39,7 @@
     streams, taps_in, residue_in, rate_in, skip_in, q_in, k_in, v_in,
     hy_v, at_v,
     taps, residue, rate, skip,
-    xs, qv, kv, rim_tx, rim_rx, ext, gated, mixed, tapx, falls, decay, coeff, toep, longt, gate,
+    xs, qv, kv, rim_tx, rim_rx, ext, gated, mixed, rates, residues, skips, tapx, falls, decay, coeff, longt, gate,
     st_tx, st_rx, acc, big,
     in_sem, kv_send, kv_recv, rim_send, rim_recv, st_send, st_recv,
 ):
@@ -122,45 +122,56 @@
     mixed[...] = jnp.zeros(mixed.shape, F32)
     for j in range(3):
         mixed[EDGE * j:EDGE * j + reach + 1, :] = taps[j]
-    mixed[3 * EDGE:, :] = rate[...]
+    mixed[3 * EDGE:3 * EDGE + modes, :] = rate[...]
+    mixed[3 * EDGE + modes:, :] = residue[...]
     whole = mixed[...]
     high, rest = split_f32(whole)
     middle, rest = split_f32(rest)
-    count = 3 * EDGE + modes
+    count = 3 * EDGE + 2 * modes
     spread_out = dot(jnp.concatenate([high, middle, rest], axis=0).astype(BF16), spread)
     spread_out = (spread_out[2 * count:] + spread_out[count:2 * count]) + spread_out[:count]
     for j in range(3):
         tapx[j] = spread_out[EDGE * j:EDGE * (j + 1)]
-    rate_nc = spread_out[3 * EDGE:]
+    rate_nc = spread_out[3 * EDGE:3 * EDGE + modes]
+    rates[...] = rate_nc
+    residues[...] = spread_out[3 * EDGE + modes:]
     step_decay = jnp.exp(rate_nc * (-float(rows)))
 
-    for j in range(3):
-        for q in range(tiles):
-            ext[j * tiles + q, EDGE:, :] = xs[j, :, q * LANES:(q + 1) * LANES].astype(F32)
+    for q in range(tiles):
+        skips[:1, q * LANES:(q + 1) * LANES] = skip[q * LANES:(q + 1) * LANES].reshape(1, LANES)
+
+    def lanes_of(q):
+        if isinstance(q, int):
+            return pl.ds(q * LANES, LANES)
+        return pl.ds(pl.multiple_of(q * LANES, LANES), LANES)
 
     def filtered(j, q, low, high):
         total = None
         for k in range(reach + 1):
-            term = (tapx[j, k:k + 1, q * LANES:(q + 1) * LANES]
+            term = (tapx[j, k:k + 1, lanes_of(q)]
                     * ext[j * tiles + q, pl.ds(EDGE - k + low, high - low), :])
             total = term if total is None else total + term
         return total
 
-    def fill_gated(low, high):
-        for q in range(tiles):
-            gated[low:high, q * LANES:(q + 1) * LANES] = (
-                filtered(1, q, low, high) * filtered(2, q, low, high)).astype(BF16)
-
-    fill_gated(HEAD_ROWS, rows)
+    def fill_gated(q, low, high):
+        gated[low:high, lanes_of(q)] = (
+            filtered(1, q, low, high) * filtered(2, q, low, high)).astype(BF16)
 
     lane = iota((modes, LANES), 1).astype(F32)
-    rate_v = rate[...]
-    for g in range(groups):
-        rate_b = jnp.broadcast_to(rate_v[:, g:g + 1], (modes, LANES))
-        fall = jnp.exp(rate_b * (lane - (rows - 1.0)))
-        q, gg = g // per, g % per
-        falls[q, gg * modes:(gg + 1) * modes, :] = fall
-        decay[q, gg * modes:(gg + 1) * modes, :] = fall.astype(BF16)
+
+    def prepare(q, carry):
+        for j in range(3):
+            ext[j * tiles + q, EDGE:, :] = xs[j, :, lanes_of(q)].astype(F32)
+        fill_gated(q, HEAD_ROWS, rows)
+        rate_v = rates[:, lanes_of(q)]
+        for gg in range(per):
+            rate_b = jnp.broadcast_to(rate_v[:, gg * GSIZE:gg * GSIZE + 1], (modes, LANES))
+            fall = jnp.exp(rate_b * (lane - (rows - 1.0)))
+            falls[q, gg * modes:(gg + 1) * modes, :] = fall
+            decay[q, gg * modes:(gg + 1) * modes, :] = fall.astype(BF16)
+        return carry
+
+    lax.fori_loop(0, tiles, prepare, 0)
 
     @pl.when(me > 0)
     def _():
@@ -177,7 +188,8 @@
     def _():
         ext[:, :EDGE, :] = jnp.zeros((3 * tiles, EDGE, LANES), F32)
 
-    fill_gated(0, HEAD_ROWS)
+    for q in range(tiles):
+        fill_gated(q, 0, HEAD_ROWS)
 
     pick = iota((modes, LANES), 1) // GSIZE
     for q in range(tiles):
@@ -195,46 +207,48 @@
 
     half_rows = rows // 2
     causal = iota((half_rows, LANES), 1) <= iota((half_rows, LANES), 0) + half_rows
-    residue_v = residue[...]
-    for q in range(tiles):
-        turned = []
+    picks = [(iota((1, 2 * LANES), 1) % LANES // GSIZE == gg).astype(F32).astype(BF16)
+             for gg in range(per)]
+    blank = jnp.zeros((half_rows, LANES), BF16)
+
+    def forward(k, carry):
+        source = me - 2 * k
+        kv_arrival(0, source).wait_recv()
+        kv_arrival(1, source).wait_recv()
+        kv_each(source, False, lambda copy: copy.start())
+        return carry
+
+    def near_tile(q, carry):
+        @pl.when((q == tiles - 2) & (me < n - 1))
+        def _():
+            lax.fori_loop(1, me // 2 + 1, forward, 0)
+
+        rate_v = rates[:, lanes_of(q)]
+        residue_v = residues[:, lanes_of(q)]
+        turned, blocks = [], []
         for gg in range(per):
-            g = q * per + gg
-            rate_b = jnp.broadcast_to(rate_v[:, g:g + 1], (modes, LANES))
-            residue_b = jnp.broadcast_to(residue_v[:, g:g + 1], (modes, LANES))
+            one = slice(gg * GSIZE, gg * GSIZE + 1)
+            rate_b = jnp.broadcast_to(rate_v[:, one], (modes, LANES))
+            residue_b = jnp.broadcast_to(residue_v[:, one], (modes, LANES))
             turned.append(residue_b * jnp.exp(rate_b * (-1.0 - lane)))
             fall = falls[q, gg * modes:(gg + 1) * modes, :]
             table = jnp.sum(residue_b * fall, axis=0, keepdims=True)
             rolled = pltpu.roll(
                 jnp.broadcast_to(table, (half_rows, LANES)), half_rows + 1, 1,
                 stride=1, stride_axis=0)
-            toep[q, :, gg * LANES:(gg + 1) * LANES] = jnp.where(causal, rolled, 0.0).astype(BF16)
-        coeff[q] = jnp.transpose(jnp.concatenate(turned, axis=0)).astype(BF16)
-
-    def forward(k, carry):
-        source = me - 2 * k
-        kv_arrival(0, source).wait_recv()
-        kv_arrival(1, source).wait_recv()
-        kv_each(source, False, lambda copy: copy.start())
-        return carry
-
-    @pl.when(me < n - 1)
-    def _():
-        lax.fori_loop(1, me // 2 + 1, forward, 0)
-
-    picks = [(iota((1, 2 * LANES), 1) % LANES // GSIZE == gg).astype(F32).astype(BF16)
-             for gg in range(per)]
-    blank = jnp.zeros((half_rows, LANES), BF16)
-    for q in range(tiles):
-        cut = slice(q * LANES, (q + 1) * LANES)
-        own = gated[:, cut]
+            blocks.append(jnp.where(causal, rolled, 0.0).astype(BF16))
+        own = gated[:, lanes_of(q)]
         moved = jnp.concatenate([blank, own[:half_rows]], axis=0)
         pair = jnp.concatenate([moved, own], axis=1)
         parts = jnp.concatenate([pair * picks[gg] for gg in range(per)], axis=0)
-        near = dot(toep[q], parts)
+        near = dot(jnp.concatenate(blocks, axis=1), parts)
         near = jnp.concatenate([near[:, :LANES], near[:, LANES:]], axis=0)
-        longt[:, cut] = near + skip[cut].reshape(1, LANES) * own.astype(F32)
-        gate[:, cut] = filtered(0, q, 0, rows)
+        coeff[q] = jnp.transpose(jnp.concatenate(turned, axis=0)).astype(BF16)
+        gate[:, lanes_of(q)] = filtered(0, q, 0, rows)
+        longt[:, lanes_of(q)] = near + skips[:1, lanes_of(q)] * own.astype(F32)
+        return carry
+
+    lax.fori_loop(0, tiles, near_tile, 0)
 
     scale = math.log2(math.e) / math.sqrt(LANES)
     for copy in in_copies[1:4]:
@@ -279,9 +293,6 @@
             acc[:, cut] = acc[:, cut] * fix + dot(value, weights)[:last]
         return carry
 
-    middle_block = jnp.maximum(me, jnp.minimum(me + 1, 2))
-    lax.fori_loop(1, middle_block, far_block, 0)
-
     def gather_state(source, state):
         st_arrival(source).wait_recv()
         return state * step_decay + st_rx[source].astype(F32)
@@ -294,7 +305,7 @@
         far = dot(coeff[q], block.astype(BF16))
         hy_v[:, cut] = (gate[:, cut] * (longt[:, cut] + far)).astype(BF16)
 
-    lax.fori_loop(middle_block, me + 1, far_block, 0)
+    lax.fori_loop(1, me + 1, far_block, 0)
 
     for c in range(wide // LANES):
         cut = slice(c * LANES, (c + 1) * LANES)
@@ -357,12 +368,14 @@
             pltpu.VMEM((2 * EDGE, chans + chans // 2), BF16),
             pltpu.VMEM((3 * tiles, rows + EDGE, LANES), F32),
             pltpu.VMEM((rows, chans), BF16),
-            pltpu.VMEM((3 * EDGE + modes, groups), F32),
+            pltpu.VMEM((3 * EDGE + 2 * modes, groups), F32),
+            pltpu.VMEM((modes, chans), F32),
+            pltpu.VMEM((modes, chans), F32),
+            pltpu.VMEM((EDGE, chans), F32),
             pltpu.VMEM((3, EDGE, chans), F32),
             pltpu.VMEM((tiles, LANES, LANES), F32),
             pltpu.VMEM((tiles, LANES, LANES), BF16),
             pltpu.VMEM((tiles, LANES, LANES), BF16),
-            pltpu.VMEM((tiles, rows // 2, per * LANES), BF16),
             pltpu.VMEM((rows, chans), F32),
             pltpu.VMEM((rows, chans), F32),
             pltpu.VMEM((modes, chans), BF16),

time: 14.2 us -> 15 us (1.056)
  Pallas kernels: 13.4 us -> 14.2 us
    pallas_call x1, Pallas kernels: 12.6 us -> 13.4 us  [body(): pl.pallas_call(functools.partial(kernel, n, heads, chunk), out_shape=(jax...]
where the time goes in v6:
time: 15 us; the launch traced here: 14.8 us
  Pallas kernels  14.2 us (95%)
  between operations  0.64 us (4%)
    pallas_call x1, Pallas kernels, body(): pl.pallas_call(functools.partial(kernel, n, heads, chunk), out_shape=(jax...  13.4 us
    pallas_call x1, Pallas kernels, body(): pl.pallas_call(leave, out_shape=(jax.ShapeDtypeStruct((rows, chans), BF16...  0.79 us

profile of v6, /device:TPU:24, one launch (start us, length us, event | category | flops | bytes accessed | tf_op | source)
XLA Modules:
  0.0 14.8 jit_solution(17042507562163498800)
XLA Ops:
  0.6 13.4 %mixers.1 = (bf16[128,768]{1,0:T(8,128)(2,1)S(1)}, bf16[1024,128]{1,0:T(8,128)(2,1)S(1)}) custom-call(bf16[3,128,768]{2,1,0:T(8,128)(2,1)} %bitcast.6, f32[3,7,48]{2,1,0:T(8,128)} %bitcast.10, f32[16,48]{1,0:T(8,128)} %residue_in.1, f32[16,48]{1,0:T(8,128)} %rate_in.1, f32[768]{0:T(1024)} %skip_in.1, bf16[1024,128]{1,0:T(8,128)(2,1)} %bitcast.7, ...), custom_call_target="tpu_custom_call" | custom-call | tf_op jit(solution)/shard_map/mixers/pallas_call | solution.py:353
  14.0 0.8 %leave.1 = (bf16[128,768]{1,0:T(8,128)(2,1)}, bf16[1024,128]{1,0:T(8,128)(2,1)}) custom-call(bf16[128,768]{1,0:T(8,128)(2,1)S(1)} %get-tuple-element.6.hy_v, bf16[1024,128]{1,0:T(8,128)(2,1)S(1)} %get-tuple-element.7.at_v), custom_call_target="tpu_custom_call" | custom-call | tf_op jit(solution)/shard_map/leave/pallas_call | solution.py:401

commit v7 on v6

--- a/solution.py
+++ b/solution.py
@@ -70,22 +70,22 @@
         def _():
             pl.semaphore_signal(barrier, inc=1, device_id={"ctx": me - d}, device_id_type=MESH)
 
-    def kv_copy(part, source, d, own=False):
-        src = (k_in if part == 0 else v_in) if own else kv.at[source, part]
+    def kv_copy(part, d):
         return pltpu.make_async_remote_copy(
-            src_ref=src, dst_ref=kv.at[source, part], send_sem=kv_send.at[source, d - 1, part],
-            recv_sem=kv_recv.at[source, part], device_id={"ctx": me + d}, device_id_type=MESH)
-
-    def kv_each(source, own, act):
-        for d in (2, 1):
+            src_ref=k_in if part == 0 else v_in, dst_ref=kv.at[me, part],
+            send_sem=kv_send.at[d, part], recv_sem=kv_recv.at[me, part],
+            device_id={"ctx": me + d}, device_id_type=MESH)
+
+    def kv_each(distances, act):
+        for d in distances:
             @pl.when(me + d < n)
             def _():
-                act(kv_copy(0, source, d, own))
-                act(kv_copy(1, source, d, own))
+                act(kv_copy(0, d))
+                act(kv_copy(1, d))
 
     def kv_arrival(part, source):
         return pltpu.make_async_remote_copy(
-            src_ref=kv.at[source, part], dst_ref=kv.at[source, part], send_sem=kv_send.at[source, 0, part],
+            src_ref=kv.at[source, part], dst_ref=kv.at[source, part], send_sem=kv_send.at[0, part],
             recv_sem=kv_recv.at[source, part], device_id={"ctx": source}, device_id_type=MESH)
 
     def st_copy(d):
@@ -103,6 +103,12 @@
             src_ref=rim_tx, dst_ref=rim_rx, send_sem=rim_send, recv_sem=rim_recv,
             device_id={"ctx": lax.rem(me + 1, n)}, device_id_type=MESH)
 
+    @pl.when(me < n - 1)
+    def _():
+        pl.semaphore_wait(barrier, n - 1 - me)
+
+    kv_each(range(n - 1, 1, -1), lambda copy: copy.start())
+
     in_copies[0].wait()
     tail = xs[:, rows - HEAD_ROWS:, :].astype(F32)[:, HEAD_ROWS - EDGE:, :]
     rim_tx[:, :chans] = jnp.concatenate([tail[1], tail[2]], axis=0).astype(BF16)
@@ -110,10 +116,9 @@
 
     @pl.when(me < n - 1)
     def _():
-        pl.semaphore_wait(barrier, n - 1 - me)
         rim_copy().start()
 
-    kv_each(me, True, lambda copy: copy.start())
+    kv_each((1,), lambda copy: copy.start())
 
     for copy in in_copies[4:]:
         copy.wait()
@@ -211,18 +216,7 @@
              for gg in range(per)]
     blank = jnp.zeros((half_rows, LANES), BF16)
 
-    def forward(k, carry):
-        source = me - 2 * k
-        kv_arrival(0, source).wait_recv()
-        kv_arrival(1, source).wait_recv()
-        kv_each(source, False, lambda copy: copy.start())
-        return carry
-
     def near_tile(q, carry):
-        @pl.when((q == tiles - 2) & (me < n - 1))
-        def _():
-            lax.fori_loop(1, me // 2 + 1, forward, 0)
-
         rate_v = rates[:, lanes_of(q)]
         residue_v = residues[:, lanes_of(q)]
         turned, blocks = [], []
@@ -276,11 +270,8 @@
     def far_block(d, carry):
         source = me - d
 
-        @pl.when((lax.rem(d, 2) == 1) | (me == n - 1))
-        def _():
-            kv_arrival(0, source).wait_recv()
-            kv_arrival(1, source).wait_recv()
-
+        kv_arrival(0, source).wait_recv()
+        kv_arrival(1, source).wait_recv()
         value = values_of(source)
         for c in range(wide // chunk):
             cut = slice(c * chunk, (c + 1) * chunk)
@@ -293,6 +284,8 @@
             acc[:, cut] = acc[:, cut] * fix + dot(value, weights)[:last]
         return carry
 
+    lax.fori_loop(1, me + 1, far_block, 0)
+
     def gather_state(source, state):
         st_arrival(source).wait_recv()
         return state * step_decay + st_rx[source].astype(F32)
@@ -305,7 +298,6 @@
         far = dot(coeff[q], block.astype(BF16))
         hy_v[:, cut] = (gate[:, cut] * (longt[:, cut] + far)).astype(BF16)
 
-    lax.fori_loop(1, me + 1, far_block, 0)
 
     for c in range(wide // LANES):
         cut = slice(c * LANES, (c + 1) * LANES)
@@ -321,13 +313,7 @@
         def _():
             st_copy(d).wait_send()
 
-    kv_each(me, True, lambda copy: copy.wait_send())
-
-    def forwarded(k, carry):
-        kv_each(me - 2 * k, False, lambda copy: copy.wait_send())
-        return carry
-
-    lax.fori_loop(1, me // 2 + 1, forwarded, 0)
+    kv_each(range(1, n), lambda copy: copy.wait_send())
 
 
 def leave(hy_v, at_v, hy_out, at_out, sem):
@@ -382,7 +368,7 @@
             pltpu.VMEM((n, modes, chans), BF16),
             pltpu.VMEM((size + EDGE, wide), F32),
             pltpu.VMEM((EDGE, wide), F32),
-            dma((8,)), dma((n, 2, 2)), dma((n, 2)),
+            dma((8,)), dma((n, 2)), dma((n, 2)),
             dma, dma, dma((n,)), dma((n,)),
         ],
         compiler_params=pltpu.CompilerParams(

time: 15 us -> 16.8 us (1.12)
  the two profiles are of different devices: /device:TPU:24 before, /device:TPU:18 now
where the time goes in v7:
time: 16.8 us; the launch traced here: 16.6 us
  Pallas kernels  16 us (95%)
  between operations  0.64 us (4%)
    pallas_call x1, Pallas kernels, body(): pl.pallas_call(functools.partial(kernel, n, heads, chunk), out_shape=(jax...  15.2 us
    pallas_call x1, Pallas kernels, body(): pl.pallas_call(leave, out_shape=(jax.ShapeDtypeStruct((rows, chans), BF16...  0.79 us

profile of v7, /device:TPU:18, one launch (start us, length us, event | category | flops | bytes accessed | tf_op | source)
XLA Modules:
  0.0 16.6 jit_solution(16685297401505554280)
XLA Ops:
  0.6 15.2 %mixers.1 = (bf16[128,768]{1,0:T(8,128)(2,1)S(1)}, bf16[1024,128]{1,0:T(8,128)(2,1)S(1)}) custom-call(bf16[3,128,768]{2,1,0:T(8,128)(2,1)} %bitcast.6, f32[3,7,48]{2,1,0:T(8,128)} %bitcast.10, f32[16,48]{1,0:T(8,128)} %residue_in.1, f32[16,48]{1,0:T(8,128)} %rate_in.1, f32[768]{0:T(1024)} %skip_in.1, bf16[1024,128]{1,0:T(8,128)(2,1)} %bitcast.7, ...), custom_call_target="tpu_custom_call" | custom-call | tf_op jit(solution)/shard_map/mixers/pallas_call | solution.py:339
  15.8 0.8 %leave.1 = (bf16[128,768]{1,0:T(8,128)(2,1)}, bf16[1024,128]{1,0:T(8,128)(2,1)}) custom-call(bf16[128,768]{1,0:T(8,128)(2,1)S(1)} %get-tuple-element.6.hy_v, bf16[1024,128]{1,0:T(8,128)(2,1)S(1)} %get-tuple-element.7.at_v), custom_call_target="tpu_custom_call" | custom-call | tf_op jit(solution)/shard_map/leave/pallas_call | solution.py:387

commit v8 on v7

--- a/solution.py
+++ b/solution.py
@@ -40,7 +40,7 @@
     hy_v, at_v,
     taps, residue, rate, skip,
     xs, qv, kv, rim_tx, rim_rx, ext, gated, mixed, rates, residues, skips, tapx, falls, decay, coeff, longt, gate,
-    st_tx, st_rx, acc, big,
+    st_tx, st_rx, run_p, run_e, acc, big,
     in_sem, kv_send, kv_recv, rim_send, rim_recv, st_send, st_recv,
 ):
     me = lax.axis_index("ctx")
@@ -70,45 +70,48 @@
         def _():
             pl.semaphore_signal(barrier, inc=1, device_id={"ctx": me - d}, device_id_type=MESH)
 
-    def kv_copy(part, d):
+    def kv_copy(part, source, own):
+        src = (k_in if part == 0 else v_in) if own else kv.at[source, part]
         return pltpu.make_async_remote_copy(
-            src_ref=k_in if part == 0 else v_in, dst_ref=kv.at[me, part],
-            send_sem=kv_send.at[d, part], recv_sem=kv_recv.at[me, part],
-            device_id={"ctx": me + d}, device_id_type=MESH)
-
-    def kv_each(distances, act):
-        for d in distances:
-            @pl.when(me + d < n)
-            def _():
-                act(kv_copy(0, d))
-                act(kv_copy(1, d))
+            src_ref=src, dst_ref=kv.at[source, part], send_sem=kv_send.at[source, part],
+            recv_sem=kv_recv.at[source, part], device_id={"ctx": lax.rem(me + 1, n)},
+            device_id_type=MESH)
 
     def kv_arrival(part, source):
         return pltpu.make_async_remote_copy(
-            src_ref=kv.at[source, part], dst_ref=kv.at[source, part], send_sem=kv_send.at[0, part],
+            src_ref=kv.at[source, part], dst_ref=kv.at[source, part], send_sem=kv_send.at[source, part],
             recv_sem=kv_recv.at[source, part], device_id={"ctx": source}, device_id_type=MESH)
 
-    def st_copy(d):
+    steps = (n - 1).bit_length()
+
+    def st_copy(k):
         return pltpu.make_async_remote_copy(
-            src_ref=st_tx, dst_ref=st_rx.at[me], send_sem=st_send.at[d],
-            recv_sem=st_recv.at[me], device_id={"ctx": me + d}, device_id_type=MESH)
-
-    def st_arrival(source):
-        return pltpu.make_async_remote_copy(
-            src_ref=st_tx, dst_ref=st_rx.at[source], send_sem=st_send.at[0],
-            recv_sem=st_recv.at[source], device_id={"ctx": source}, device_id_type=MESH)
+            src_ref=st_tx.at[k], dst_ref=st_rx.at[k], send_sem=st_send.at[k],
+            recv_sem=st_recv.at[k], device_id={"ctx": lax.rem(me + 2 ** k, n)},
+            device_id_type=MESH)
+
+    def st_out(k):
+        st_tx[k] = run_p[...].astype(BF16)
+
+        @pl.when(me + 2 ** k < n)
+        def _():
+            st_copy(k).start()
+
+    def st_in(k):
+        @pl.when(me >= 2 ** k)
+        def _():
+            st_copy(k).wait_recv()
+            got = st_rx[k].astype(F32)
+            fall = -float(rows) * rates[...]
+            run_e[...] += got if k == 0 else got * jnp.exp(fall * (2 ** k - 1.0))
+            if k + 1 < steps:
+                run_p[...] += got * jnp.exp(fall * float(2 ** k))
 
     def rim_copy():
         return pltpu.make_async_remote_copy(
             src_ref=rim_tx, dst_ref=rim_rx, send_sem=rim_send, recv_sem=rim_recv,
             device_id={"ctx": lax.rem(me + 1, n)}, device_id_type=MESH)
 
-    @pl.when(me < n - 1)
-    def _():
-        pl.semaphore_wait(barrier, n - 1 - me)
-
-    kv_each(range(n - 1, 1, -1), lambda copy: copy.start())
-
     in_copies[0].wait()
     tail = xs[:, rows - HEAD_ROWS:, :].astype(F32)[:, HEAD_ROWS - EDGE:, :]
     rim_tx[:, :chans] = jnp.concatenate([tail[1], tail[2]], axis=0).astype(BF16)
@@ -116,9 +119,13 @@
 
     @pl.when(me < n - 1)
     def _():
+        pl.semaphore_wait(barrier, n - 1 - me)
         rim_copy().start()
 
-    kv_each((1,), lambda copy: copy.start())
+    @pl.when(me < n - 1)
+    def _():
+        kv_copy(0, me, True).start()
+        kv_copy(1, me, True).start()
 
     for copy in in_copies[4:]:
         copy.wait()
@@ -140,7 +147,6 @@
     rate_nc = spread_out[3 * EDGE:3 * EDGE + modes]
     rates[...] = rate_nc
     residues[...] = spread_out[3 * EDGE + modes:]
-    step_decay = jnp.exp(rate_nc * (-float(rows)))
 
     for q in range(tiles):
         skips[:1, q * LANES:(q + 1) * LANES] = skip[q * LANES:(q + 1) * LANES].reshape(1, LANES)
@@ -203,12 +209,9 @@
         state = jnp.zeros((modes, LANES), F32)
         for gg in range(per):
             state = jnp.where(pick == gg, full[gg * modes:(gg + 1) * modes], state)
-        st_tx[:, cut] = state.astype(BF16)
-
-    for d in range(1, n):
-        @pl.when(me + d < n)
-        def _():
-            st_copy(d).start()
+        run_p[:, cut] = state
+    run_e[...] = jnp.zeros(run_e.shape, F32)
+    st_out(0)
 
     half_rows = rows // 2
     causal = iota((half_rows, LANES), 1) <= iota((half_rows, LANES), 0) + half_rows
@@ -216,7 +219,16 @@
              for gg in range(per)]
     blank = jnp.zeros((half_rows, LANES), BF16)
 
+    def pass_on(source):
+        for part in range(2):
+            kv_arrival(part, source).wait_recv()
+            kv_copy(part, source, False).start()
+
     def near_tile(q, carry):
+        @pl.when((q == tiles - 2) & (me > 0) & (me < n - 1))
+        def _():
+            pass_on(me - 1)
+
         rate_v = rates[:, lanes_of(q)]
         residue_v = residues[:, lanes_of(q)]
         turned, blocks = [], []
@@ -244,6 +256,12 @@
 
     lax.fori_loop(0, tiles, near_tile, 0)
 
+    for k in range(steps - 1):
+        @pl.when(me + 2 ** (k + 1) < n)
+        def _():
+            st_in(k)
+            st_out(k + 1)
+
     scale = math.log2(math.e) / math.sqrt(LANES)
     for copy in in_copies[1:4]:
         copy.wait()
@@ -270,8 +288,15 @@
     def far_block(d, carry):
         source = me - d
 
-        kv_arrival(0, source).wait_recv()
-        kv_arrival(1, source).wait_recv()
+        @pl.when((me < n - 1) & (d < me))
+        def _():
+            pass_on(source - 1)
+
+        @pl.when(me == n - 1)
+        def _():
+            kv_arrival(0, source).wait_recv()
+            kv_arrival(1, source).wait_recv()
+
         value = values_of(source)
         for c in range(wide // chunk):
             cut = slice(c * chunk, (c + 1) * chunk)
@@ -284,20 +309,22 @@
             acc[:, cut] = acc[:, cut] * fix + dot(value, weights)[:last]
         return carry
 
-    lax.fori_loop(1, me + 1, far_block, 0)
-
-    def gather_state(source, state):
-        st_arrival(source).wait_recv()
-        return state * step_decay + st_rx[source].astype(F32)
-
-    state = lax.fori_loop(0, me, gather_state, jnp.zeros((modes, chans), F32))
+    middle = jnp.maximum(me, jnp.minimum(me + 1, 2))
+    lax.fori_loop(1, middle, far_block, 0)
+
+    for k in range(steps):
+        @pl.when(me + 2 ** (k + 1) >= n)
+        def _():
+            st_in(k)
+
     for q in range(tiles):
         cut = slice(q * LANES, (q + 1) * LANES)
         block = jnp.concatenate(
-            [jnp.where(pick == gg, state[:, cut], 0.0) for gg in range(per)], axis=0)
+            [jnp.where(pick == gg, run_e[:, cut], 0.0) for gg in range(per)], axis=0)
         far = dot(coeff[q], block.astype(BF16))
         hy_v[:, cut] = (gate[:, cut] * (longt[:, cut] + far)).astype(BF16)
 
+    lax.fori_loop(middle, me + 1, far_block, 0)
 
     for c in range(wide // LANES):
         cut = slice(c * LANES, (c + 1) * LANES)
@@ -308,12 +335,21 @@
     def _():
         rim_copy().wait_send()
 
-    for d in range(1, n):
-        @pl.when(me + d < n)
-        def _():
-            st_copy(d).wait_send()
-
-    kv_each(range(1, n), lambda copy: copy.wait_send())
+    for k in range(steps):
+        @pl.when(me + 2 ** k < n)
+        def _():
+            st_copy(k).wait_send()
+
+    def sent(source, carry):
+        kv_copy(0, source, False).wait_send()
+        kv_copy(1, source, False).wait_send()
+        return carry
+
+    @pl.when(me < n - 1)
+    def _():
+        kv_copy(0, me, True).wait_send()
+        kv_copy(1, me, True).wait_send()
+        lax.fori_loop(0, me, sent, 0)
 
 
 def leave(hy_v, at_v, hy_out, at_out, sem):
@@ -334,6 +370,7 @@
     wide = heads * rows
     chunk = min(256, wide)
     reach = short_taps.shape[0]
+    steps = (n - 1).bit_length()
     vmem, hbm = pl.BlockSpec(memory_space=pltpu.VMEM), pl.BlockSpec(memory_space=pltpu.HBM)
     dma = pltpu.SemaphoreType.DMA
     hyena, attn = pl.pallas_call(
@@ -364,12 +401,14 @@
             pltpu.VMEM((tiles, LANES, LANES), BF16),
             pltpu.VMEM((rows, chans), F32),
             pltpu.VMEM((rows, chans), F32),
-            pltpu.VMEM((modes, chans), BF16),
-            pltpu.VMEM((n, modes, chans), BF16),
+            pltpu.VMEM((steps, modes, chans), BF16),
+            pltpu.VMEM((steps, modes, chans), BF16),
+            pltpu.VMEM((modes, chans), F32),
+            pltpu.VMEM((modes, chans), F32),
             pltpu.VMEM((size + EDGE, wide), F32),
             pltpu.VMEM((EDGE, wide), F32),
             dma((8,)), dma((n, 2)), dma((n, 2)),
-            dma, dma, dma((n,)), dma((n,)),
+            dma, dma, dma((steps,)), dma((steps,)),
         ],
         compiler_params=pltpu.CompilerParams(
             collective_id=0, has_side_effects=True, vmem_limit_bytes=40 * 1024 * 1024),

time: 16.8 us -> 15.7 us (0.935)
  the two profiles are of different devices: /device:TPU:18 before, /device:TPU:24 now
where the time goes in v8:
time: 15.7 us; the launch traced here: 15.6 us
  Pallas kernels  15 us (96%)
  between operations  0.64 us (4%)
    pallas_call x1, Pallas kernels, body(): pl.pallas_call(functools.partial(kernel, n, heads, chunk), out_shape=(jax...  14.2 us
    pallas_call x1, Pallas kernels, body(): pl.pallas_call(leave, out_shape=(jax.ShapeDtypeStruct((rows, chans), BF16...  0.79 us

profile of v8, /device:TPU:24, one launch (start us, length us, event | category | flops | bytes accessed | tf_op | source)
XLA Modules:
  0.0 15.6 jit_solution(10488591239215311969)
XLA Ops:
  0.6 14.2 %mixers.1 = (bf16[128,768]{1,0:T(8,128)(2,1)S(1)}, bf16[1024,128]{1,0:T(8,128)(2,1)S(1)}) custom-call(bf16[3,128,768]{2,1,0:T(8,128)(2,1)} %bitcast.6, f32[3,7,48]{2,1,0:T(8,128)} %bitcast.10, f32[16,48]{1,0:T(8,128)} %residue_in.1, f32[16,48]{1,0:T(8,128)} %rate_in.1, f32[768]{0:T(1024)} %skip_in.1, bf16[1024,128]{1,0:T(8,128)(2,1)} %bitcast.7, ...), custom_call_target="tpu_custom_call" | custom-call | tf_op jit(solution)/shard_map/mixers/pallas_call | solution.py:376
  14.8 0.8 %leave.1 = (bf16[128,768]{1,0:T(8,128)(2,1)}, bf16[1024,128]{1,0:T(8,128)(2,1)}) custom-call(bf16[128,768]{1,0:T(8,128)(2,1)S(1)} %get-tuple-element.6.hy_v, bf16[1024,128]{1,0:T(8,128)(2,1)S(1)} %get-tuple-element.7.at_v), custom_call_target="tpu_custom_call" | custom-call | tf_op jit(solution)/shard_map/leave/pallas_call | solution.py:426

commit v9 on v6

--- a/solution.py
+++ b/solution.py
@@ -293,6 +293,9 @@
             acc[:, cut] = acc[:, cut] * fix + dot(value, weights)[:last]
         return carry
 
+    middle = jnp.maximum(me, jnp.minimum(me + 1, 2))
+    lax.fori_loop(1, middle, far_block, 0)
+
     def gather_state(source, state):
         st_arrival(source).wait_recv()
         return state * step_decay + st_rx[source].astype(F32)
@@ -305,7 +308,7 @@
         far = dot(coeff[q], block.astype(BF16))
         hy_v[:, cut] = (gate[:, cut] * (longt[:, cut] + far)).astype(BF16)
 
-    lax.fori_loop(1, me + 1, far_block, 0)
+    lax.fori_loop(middle, me + 1, far_block, 0)
 
     for c in range(wide // LANES):
         cut = slice(c * LANES, (c + 1) * LANES)

time: 15 us -> 13.8 us (0.920)
  the two profiles are of different devices: /device:TPU:24 before, /device:TPU:16 now
where the time goes in v9:
time: 13.8 us; the launch traced here: 13.6 us
  Pallas kernels  13 us (94%)
  between operations  0.64 us (5%)
    pallas_call x1, Pallas kernels, body(): pl.pallas_call(functools.partial(kernel, n, heads, chunk), out_shape=(jax...  12.2 us
    pallas_call x1, Pallas kernels, body(): pl.pallas_call(leave, out_shape=(jax.ShapeDtypeStruct((rows, chans), BF16...  0.79 us

profile of v9, /device:TPU:16, one launch (start us, length us, event | category | flops | bytes accessed | tf_op | source)
XLA Modules:
  0.0 13.6 jit_solution(6052016670536846885)
XLA Ops:
  0.6 12.2 %mixers.1 = (bf16[128,768]{1,0:T(8,128)(2,1)S(1)}, bf16[1024,128]{1,0:T(8,128)(2,1)S(1)}) custom-call(bf16[3,128,768]{2,1,0:T(8,128)(2,1)} %bitcast.6, f32[3,7,48]{2,1,0:T(8,128)} %bitcast.10, f32[16,48]{1,0:T(8,128)} %residue_in.1, f32[16,48]{1,0:T(8,128)} %rate_in.1, f32[768]{0:T(1024)} %skip_in.1, bf16[1024,128]{1,0:T(8,128)(2,1)} %bitcast.7, ...), custom_call_target="tpu_custom_call" | custom-call | tf_op jit(solution)/shard_map/mixers/pallas_call | solution.py:356
  12.8 0.8 %leave.1 = (bf16[128,768]{1,0:T(8,128)(2,1)}, bf16[1024,128]{1,0:T(8,128)(2,1)}) custom-call(bf16[128,768]{1,0:T(8,128)(2,1)S(1)} %get-tuple-element.6.hy_v, bf16[1024,128]{1,0:T(8,128)(2,1)S(1)} %get-tuple-element.7.at_v), custom_call_target="tpu_custom_call" | custom-call | tf_op jit(solution)/shard_map/leave/pallas_call | solution.py:404
